TPU v7x, 32 devices: a whole 2x2x4 slice. The times are simulated.
32 devices in a mesh: shot: 2 (over x), gx: 16 (over z, y, core).
Axes of the slice: x: 2, y: 2, z: 4, core: 2. Of those that a mesh axis runs over, the one named last changes fastest.
Arguments:
- source_field: float32 [512, 16, 128], P(('shot', 'gx')), parts along dimension 0, may hold values from -6 to 6
- source_prior: float32 [512, 16, 128], P(('shot', 'gx')), parts along dimension 0, may hold values from -6 to 6
- receiver_field: float32 [512, 16, 128], P(('shot', 'gx')), parts along dimension 0, may hold values from -6 to 6
- receiver_prior: float32 [512, 16, 128], P(('shot', 'gx')), parts along dimension 0, may hold values from -6 to 6
- stiffness: float32 [256, 16, 128], P('gx'), may hold values from 0.02 to 0.085
- buoyancy: float32 [256, 16, 128], P('gx'), may hold values from 0.5 to 2
- wavelet: float32 [32, 8], P('shot'), parts along dimension 0, may hold values from -6 to 6
- fire_step: int32 [32], P('shot'), parts along dimension 0, may hold values from 0 to 7
- shot_cell: int32 [32], P('shot'), parts along dimension 0, may hold values from 0 to 4095
- receiver_cell: int32 [4096], P('shot'), parts along dimension 0, may hold values from 0 to 4095
- traces: float32 [16, 2048], P('shot', 'gx'), parts along dimension 0, may hold values from -6 to 6
Outputs:
- image_sum: float32 [66, 256, 16, 128], P('shot', 'gx'), parts along dimension 0
There are 2 independent parts, one for each index of `shot`. A program takes and returns all parts, laid end to end along the dimension named above; an argument that names none is the same for every part. Nothing has to cross between parts.
All inputs are finite; a program needn't handle non-finite values.
Results may differ from a plain program's by a relative error of at most 0.0003.
Values sent between devices are 32-bit elements; how exact they have to be, the bound alone decides.
A program may use at most 64 MiB of HBM per device.

v0:
```python
import jax
import jax.numpy as jnp
from jax import lax
from jax.sharding import PartitionSpec as P

STEPS = 8
IMG_EVERY = 4
NOFF = 33
SURFACE = 4
HALF = 16


stencil_weights = (1.6, -0.2, 8.0 / 315.0, -1.0 / 560.0)


def with_halo(cells, sides, width):
    for axis, dim in sides:
        count = lax.axis_size(axis)
        ends = count - 1
        head = lax.slice_in_dim(cells, 0, width, axis=dim)
        tail = lax.slice_in_dim(cells, cells.shape[dim] - width, cells.shape[dim], axis=dim)
        cells = jnp.concatenate(
            [
                lax.ppermute(tail, axis, [(i, (i + 1) % count) for i in range(ends)]),
                cells,
                lax.ppermute(head, axis, [((i + 1) % count, i) for i in range(ends)]),
            ],
            axis=dim,
        )
    return cells


def window(padded, direction, offset, extent):
    starts = [4, 4, 4]
    starts[direction] = starts[direction] + offset
    return padded[
        starts[0] : starts[0] + extent[0],
        starts[1] : starts[1] + extent[1],
        starts[2] : starts[2] + extent[2],
    ]


def laplace(wavefield, buoyant):
    extent = (wavefield.shape[0] - 8, wavefield.shape[1], wavefield.shape[2])
    padded_field = jnp.pad(wavefield, ((0, 0), (4, 4), (4, 4)))
    padded_buoyant = jnp.pad(buoyant, ((0, 0), (4, 4), (4, 4)))
    centre_field = window(padded_field, 0, 0, extent)
    centre_buoyant = window(padded_buoyant, 0, 0, extent)
    accumulated = jnp.zeros(extent, jnp.float32)
    for direction in range(3):
        for distance in range(4):
            for orientation in (1, -1):
                other_field = window(padded_field, direction, orientation * (distance + 1), extent)
                other_buoyant = window(
                    padded_buoyant, direction, orientation * (distance + 1), extent
                )
                accumulated = accumulated + stencil_weights[distance] * (
                    0.5 * (centre_buoyant + other_buoyant)
                ) * (other_field - centre_field)
    return accumulated


def plane_terms(cell_index, amounts, first_row, span_rows, lateral):
    inline = cell_index // lateral
    crossline = cell_index % lateral
    row_hot = (
        (inline - first_row)[:, None] == jnp.arange(span_rows, dtype=jnp.int32)[None, :]
    ).astype(jnp.float32)
    cross_hot = (crossline[:, None] == jnp.arange(lateral, dtype=jnp.int32)[None, :]).astype(
        jnp.float32
    )
    weighted = amounts[:, :, None] * cross_hot[None, :, :]
    return jnp.einsum("tnc,nr->trc", weighted, row_hot, precision=lax.Precision.HIGHEST)


def advance(current, prior_field, buoyant, stiff_cells, source_term):
    centre_cells = current[4 : current.shape[0] - 4]
    updated = 2.0 * centre_cells - prior_field + stiff_cells * laplace(current, buoyant)
    return updated.at[:, :, SURFACE].add(source_term)


def correlate(lag_source, lag_receiver, span_rows):
    pieces = []
    for offset_index in range(NOFF):
        lag_shift = offset_index - HALF
        pieces.append(
            lag_source[HALF - lag_shift : HALF - lag_shift + span_rows]
            * lag_receiver[HALF + lag_shift : HALF + lag_shift + span_rows]
        )
    return jnp.stack(pieces, 0)


def local(
    source_field,
    source_prior,
    receiver_field,
    receiver_prior,
    stiffness,
    buoyancy,
    wavelet,
    fire_step,
    shot_cell,
    receiver_cell,
    traces,
):
    brick_width = source_field.shape[0]
    lateral = source_field.shape[1]
    anchor = lax.axis_index("gx") * brick_width
    all_traces = lax.all_gather(traces, "gx", axis=1, tiled=True)
    wide_rows = brick_width + 2 * HALF
    reversed_traces = all_traces[::-1]
    moments = jnp.arange(STEPS, dtype=jnp.int32)
    delays = moments[:, None] - fire_step[None, :]
    choose = delays[:, :, None] == jnp.arange(wavelet.shape[1], dtype=jnp.int32)[None, None, :]
    shot_amounts = jnp.sum(jnp.where(choose, wavelet[None, :, :], 0.0), axis=2)
    shot_planes = plane_terms(shot_cell, shot_amounts, anchor - HALF, wide_rows, lateral)
    receiver_planes = plane_terms(receiver_cell, reversed_traces, anchor - HALF, wide_rows, lateral)
    wide_buoyant = with_halo(buoyancy, (("gx", 0),), HALF)
    wide_stiff = with_halo(stiffness, (("gx", 0),), HALF - 4)
    source_now, source_before = (source_field, source_prior)
    receiver_now, receiver_before = (receiver_field, receiver_prior)
    rounds = STEPS // IMG_EVERY
    image_sum = None
    for imaging_round in range(rounds + 1):
        lag_source, lag_receiver = (
            with_halo(source_now, (("gx", 0),), HALF),
            with_halo(receiver_now, (("gx", 0),), HALF),
        )
        product = correlate(lag_source, lag_receiver, brick_width)
        image_sum = product if imaging_round == 0 else image_sum + product
        if imaging_round < rounds:
            block_start = imaging_round * IMG_EVERY
            older_source, older_receiver = (
                with_halo(source_before, (("gx", 0),), HALF - 4),
                with_halo(receiver_before, (("gx", 0),), HALF - 4),
            )
            wide_source, wide_receiver = (lag_source, lag_receiver)
            for substep in range(IMG_EVERY):
                moment = block_start + substep
                margin = HALF - 4 * (substep + 1)
                extent = brick_width + 2 * margin
                cut_rows = 4 * substep
                first = HALF - margin
                buoyant_now = wide_buoyant[cut_rows : cut_rows + extent + 8]
                stiff_now = wide_stiff[cut_rows : cut_rows + extent]
                source_term = shot_planes[moment, first : first + extent]
                receiver_term = receiver_planes[moment, first : first + extent]
                source_next = advance(
                    wide_source, older_source, buoyant_now, stiff_now, source_term
                )
                receiver_next = advance(
                    wide_receiver, older_receiver, buoyant_now, stiff_now, receiver_term
                )
                previous_source, previous_receiver = (wide_source, wide_receiver)
                if substep < IMG_EVERY - 1:
                    older_source = previous_source[8 : previous_source.shape[0] - 8]
                    older_receiver = previous_receiver[8 : previous_receiver.shape[0] - 8]
                wide_source, wide_receiver = (source_next, receiver_next)
            source_before = previous_source[4 : previous_source.shape[0] - 4]
            receiver_before = previous_receiver[4 : previous_receiver.shape[0] - 4]
            source_now, receiver_now = (wide_source, wide_receiver)
    return image_sum


def solution(mesh):
    placed = (
        P(("shot", "gx"), None, None),
        P(("shot", "gx"), None, None),
        P(("shot", "gx"), None, None),
        P(("shot", "gx"), None, None),
        P("gx", None, None),
        P("gx", None, None),
        P("shot", None),
        P("shot"),
        P("shot"),
        P("shot"),
        P("shot", "gx"),
    )
    return jax.shard_map(
        local, mesh=mesh, in_specs=placed, out_specs=P("shot", "gx", None, None), check_vma=False
    )
```

profile of v0, /device:TPU:14, one launch (start us, length us, event | category | flops | bytes accessed | tf_op | source)
XLA Modules:
  0.0 241.1 jit_solution(14067689098078118635)
XLA Ops:
  2.1 3.6 %collective-permute-start.3 = (f32[16,16,128]{2,1,0:T(8,128)}, f32[16,16,128]{2,1,0:T(8,128)S(1)}, u32[]{:S(2)}, u32[]{:S(2)}) collective-permute-start(f32[16,16,128]{2,1,0:T(8,128)} %param.45), channel_id=1, source_target_pairs={{1,0},{2,1},{3,2},{4,3},{5,4},{6,5},{7,6},{8,7},{9,8},{10,9},{11,1... | collective-permute-start | bytes 393224 | tf_op jit(solution)/shard_map/ppermute | solution.py:26
  7.6 3.6 %collective-permute-start.9 = (f32[16,16,128]{2,1,0:T(8,128)}, f32[16,16,128]{2,1,0:T(8,128)S(1)}, u32[]{:S(2)}, u32[]{:S(2)}) collective-permute-start(f32[16,16,128]{2,1,0:T(8,128)} %param.48), channel_id=1, source_target_pairs={{1,0},{2,1},{3,2},{4,3},{5,4},{6,5},{7,6},{8,7},{9,8},{10,9},{11,1... | collective-permute-start | bytes 393224 | tf_op jit(solution)/shard_map/ppermute | solution.py:26
  15.7 16.5 %all_gather.3 = f32[8,2048]{1,0:T(8,128)S(1)} all-gather(f32[8,128]{1,0:T(8,128)} %param.53), channel_id=1, replica_groups=mesh['shot'=2,'gx'=16] {'gx'}, dimensions={1}, use_global_device_ids=true | all-gather | bytes 69632 | tf_op jit(solution)/shard_map/all_gather | solution.py:109
  52.8 4.3 %collective-permute-start.7 = (f32[12,16,128]{2,1,0:T(8,128)S(1)}, f32[12,16,128]{2,1,0:T(8,128)S(1)}, u32[]{:S(2)}, u32[]{:S(2)}) collective-permute-start(f32[12,16,128]{2,1,0:T(8,128)S(1)} %get-tuple-element.326), channel_id=1, source_target_pairs={{1,0},{2,1},{3,2},{4,3},{5,4},{6,5},{7,6},{8,7},{9,8},{10,9},{11,1... | collective-permute-start | bytes 294920 | tf_op jit(solution)/shard_map/ppermute | solution.py:26
  61.9 3.1 %collective-permute-start = (f32[16,16,128]{2,1,0:T(8,128)}, f32[16,16,128]{2,1,0:T(8,128)}, u32[]{:S(2)}, u32[]{:S(2)}) collective-permute-start(f32[16,16,128]{2,1,0:T(8,128)} %param.43), channel_id=1, source_target_pairs={{1,0},{2,1},{3,2},{4,3},{5,4},{6,5},{7,6},{8,7},{9,8},{10,9},{11,1... | collective-permute-start | bytes 393224 | tf_op jit(solution)/shard_map/ppermute | solution.py:26
  70.4 4.6 %collective-permute-start.5 = (f32[12,16,128]{2,1,0:T(8,128)}, f32[12,16,128]{2,1,0:T(8,128)}, u32[]{:S(2)}, u32[]{:S(2)}) collective-permute-start(f32[12,16,128]{2,1,0:T(8,128)} %get-tuple-element.316), channel_id=1, source_target_pairs={{1,0},{2,1},{3,2},{4,3},{5,4},{6,5},{7,6},{8,7},{9,8},{10,9},{11,1... | collective-permute-start | bytes 294920 | tf_op jit(solution)/shard_map/ppermute | solution.py:26
  77.1 4.3 %fusion.102 = (f32[40,16,128]{2,1,0:T(8,128)S(1)}, f32[40,16,128]{2,1,0:T(8,128)S(1)}, f32[40,16,128]{2,1,0:T(8,128)}, f32[40,16,128]{2,1,0:T(8,128)}, f32[40,16...) fusion(f32[40,16,128]{2,1,0:T(8,128)S(1)} %constant_dynamic-upd, ...), kind=kLoop, calls=%fused_computation.651 | loop fusion | flops 10240000 | bytes 15532032 | tf_op jit(solution)/shard_map/add | solution.py:78
  82.3 5.5 %scatter-add.60 = f32[40,16,128]{2,1,0:T(8,128)S(1)} dynamic-update-slice(f32[40,16,128]{2,1,0:T(8,128)S(1)} %get-tuple-element.272, f32[40,16,1]{2,1,0:T(8,128)} %slice_add_fusion.2, s32[]{:T(128)} %constant.500.clone.1, s32[]{:T(128)} %constant.500.clone.1, s32[]{:T(128)} %constant.502.clone.1) | dynamic-update-slice | bytes 5124 | tf_op jit(solution)/shard_map/scatter-add | solution.py:79
  87.8 3.6 %fusion.402 = (f32[32,16,128]{2,1,0:T(8,128)S(1)}, f32[32,16,128]{2,1,0:T(8,128)}, f32[32,16,128]{2,1,0:T(8,128)}, f32[32,16,128]{2,1,0:T(8,128)}, f32[32,16,128...) fusion(f32[40,16,128]{2,1,0:T(8,128)S(1)} %scatter-add.60, ...), kind=kLoop, calls=%fused_computation.999 | loop fusion | flops 8060928 | bytes 12451840 | tf_op jit(solution)/shard_map/add | solution.py:78
  93.9 6.3 %fusion.702 = (f32[24,16,128]{2,1,0:T(8,128)S(1)}, f32[24,16,128]{2,1,0:T(8,128)}, f32[24,16,128]{2,1,0:T(8,128)}, f32[24,16,128]{2,1,0:T(8,128)}, f32[24,16,128...) fusion(f32[32,16,128]{2,1,0:T(8,128)S(1)} %scatter-add.61, ...), kind=kLoop, calls=%fused_computation.1470 | loop fusion | flops 6045696 | bytes 9371648 | tf_op jit(solution)/shard_map/add | solution.py:78
  105.9 4.3 %fusion.52 = f32[40,16,128]{2,1,0:T(8,128)S(1)} fusion(f32[40,16,128]{2,1,0:T(8,128)S(1)} %constant_dynamic-update-slice_fusion.44, f32[40,16,128]{2,1,0:T(8,128)} %get-tuple-element.296, f32[48,16,128]{2,1,0:T(8,128)S(1)} %get-tuple-element.312, f32[40,16,128]{2,1,0:T(8,128)} %get-tuple-element.295, f32[40,16,128]{2,1,0:T(8,128)} %get-tuple-element.294, ...), kind=kLoop, calls=%fused_computation.601 | loop fusion | flops 6307840 | bytes 12189696 | tf_op jit(solution)/shard_map/add | solution.py:78
  110.4 5.3 %scatter-add.54 = f32[40,16,128]{2,1,0:T(8,128)S(1)} dynamic-update-slice(f32[40,16,128]{2,1,0:T(8,128)S(1)} %fusion.52, f32[40,16,1]{2,1,0:T(8,128)S(1)} %slice_add_fusion.3, s32[]{:T(128)} %constant.500.clone.1, s32[]{:T(128)} %constant.500.clone.1, s32[]{:T(128)} %constant.502.clone.1) | dynamic-update-slice | bytes 5124 | tf_op jit(solution)/shard_map/scatter-add | solution.py:79
  115.7 3.7 %fusion.352 = f32[32,16,128]{2,1,0:T(8,128)S(1)} fusion(f32[32,16,128]{2,1,0:T(8,128)} %get-tuple-element.271, f32[40,16,128]{2,1,0:T(8,128)S(1)} %scatter-add.54, f32[32,16,128]{2,1,0:T(8,128)} %get-tuple-element.270, f32[32,16,128]{2,1,0:T(8,128)} %get-tuple-element.269, f32[32,16,128]{2,1,0:T(8,128)} %get-tuple-element.268, ...), kind=kLoop, calls=%fused_computation.949 | loop fusion | flops 4915200 | bytes 9764864 | tf_op jit(solution)/shard_map/add | solution.py:78
  120.3 3.3 %scatter-add.55 = f32[32,16,128]{2,1,0:T(8,128)S(1)} dynamic-update-slice(f32[32,16,128]{2,1,0:T(8,128)S(1)} %fusion.352, f32[32,16,1]{2,1,0:T(8,128)} %slice_add_fusion.15, s32[]{:T(128)} %constant.500.clone.1, s32[]{:T(128)} %constant.500.clone.1, s32[]{:T(128)} %constant.502.clone.1) | dynamic-update-slice | bytes 4100 | tf_op jit(solution)/shard_map/scatter-add | solution.py:79
  123.6 3.0 %fusion.652 = f32[24,16,128]{2,1,0:T(8,128)S(1)} fusion(f32[24,16,128]{2,1,0:T(8,128)} %get-tuple-element.246, f32[32,16,128]{2,1,0:T(8,128)S(1)} %scatter-add.55, f32[24,16,128]{2,1,0:T(8,128)} %get-tuple-element.245, f32[24,16,128]{2,1,0:T(8,128)} %get-tuple-element.244, f32[24,16,128]{2,1,0:T(8,128)} %get-tuple-element.243, ...), kind=kLoop, calls=%fused_computation.1420 | loop fusion | flops 3686400 | bytes 7340032 | tf_op jit(solution)/shard_map/add | solution.py:78
  129.5 3.8 %fusion.1227 = (f32[16,16,128]{2,1,0:T(8,128)S(1)}, f32[16,16,128]{2,1,0:T(8,128)S(1)}, f32[16,16,128]{2,1,0:T(8,128)S(1)}, f32[16,16,128]{2,1,0:T(8,128)S(1)}, ...) fusion(f32[16,16,128]{2,1,0:T(8,128)S(1)} %copy-done, ...), kind=kLoop, calls=%fused_computation.2043 | loop fusion | flops 4030464 | bytes 6291456 | tf_op jit(solution)/shard_map/add | solution.py:78
  136.2 3.6 %collective-permute-start.10 = (f32[16,16,128]{2,1,0:T(8,128)S(1)}, f32[16,16,128]{2,1,0:T(8,128)S(1)}, u32[]{:S(2)}, u32[]{:S(2)}) collective-permute-start(f32[16,16,128]{2,1,0:T(8,128)S(1)} %scatter-add.59), channel_id=1, source_target_pairs={{1,0},{2,1},{3,2},{4,3},{5,4},{6,5},{7,6},{8,7},{9,8},{10,9},{11,1... | collective-permute-start | bytes 393224 | tf_op jit(solution)/shard_map/ppermute | solution.py:26
  144.6 3.6 %collective-permute-start.15 = (f32[16,16,128]{2,1,0:T(8,128)S(1)}, f32[16,16,128]{2,1,0:T(8,128)S(1)}, u32[]{:S(2)}, u32[]{:S(2)}) collective-permute-start(f32[16,16,128]{2,1,0:T(8,128)S(1)} %scatter-add.65), channel_id=1, source_target_pairs={{1,0},{2,1},{3,2},{4,3},{5,4},{6,5},{7,6},{8,7},{9,8},{10,9},{11,1... | collective-permute-start | bytes 393224 | tf_op jit(solution)/shard_map/ppermute | solution.py:26
  150.6 3.7 %collective-permute-start.17 = (f32[12,16,128]{2,1,0:T(8,128)}, f32[12,16,128]{2,1,0:T(8,128)}, u32[]{:S(2)}, u32[]{:S(2)}) collective-permute-start(f32[12,16,128]{2,1,0:T(8,128)} %get-tuple-element.300), channel_id=1, source_target_pairs={{1,0},{2,1},{3,2},{4,3},{5,4},{6,5},{7,6},{8,7},{9,8},{10,9},{11,1... | collective-permute-start | bytes 294920 | tf_op jit(solution)/shard_map/ppermute | solution.py:26
  159.0 4.5 %collective-permute-start.20 = (f32[12,16,128]{2,1,0:T(8,128)S(1)}, f32[12,16,128]{2,1,0:T(8,128)S(1)}, u32[]{:S(2)}, u32[]{:S(2)}) collective-permute-start(f32[12,16,128]{2,1,0:T(8,128)S(1)} %get-tuple-element.298), channel_id=1, source_target_pairs={{1,0},{2,1},{3,2},{4,3},{5,4},{6,5},{7,6},{8,7},{9,8},{10,9},{11,1... | collective-permute-start | bytes 294920 | tf_op jit(solution)/shard_map/ppermute | solution.py:26
  165.8 3.2 %collective-permute-start.16 = (f32[12,16,128]{2,1,0:T(8,128)}, f32[12,16,128]{2,1,0:T(8,128)}, u32[]{:S(2)}, u32[]{:S(2)}) collective-permute-start(f32[12,16,128]{2,1,0:T(8,128)} %get-tuple-element.299), channel_id=1, source_target_pairs={{0,1},{1,2},{2,3},{3,4},{4,5},{5,6},{6,7},{7,8},{8,9},{9,10},{10,1... | collective-permute-start | bytes 294920 | tf_op jit(solution)/shard_map/ppermute | solution.py:24
  172.7 5.5 %scatter-add.74 = f32[40,16,128]{2,1,0:T(8,128)S(1)} dynamic-update-slice(f32[40,16,128]{2,1,0:T(8,128)S(1)} %fusion.202, f32[40,16,1]{2,1,0:T(8,128)} %slice_add_fusion, s32[]{:T(128)} %constant.500.clone.1, s32[]{:T(128)} %constant.500.clone.1, s32[]{:T(128)} %constant.502.clone.1) | dynamic-update-slice | bytes 5124 | tf_op jit(solution)/shard_map/scatter-add | solution.py:79
  178.3 3.3 %fusion.502 = f32[32,16,128]{2,1,0:T(8,128)S(1)} fusion(f32[32,16,128]{2,1,0:T(8,128)} %get-tuple-element.271, f32[40,16,128]{2,1,0:T(8,128)S(1)} %scatter-add.74, f32[32,16,128]{2,1,0:T(8,128)} %get-tuple-element.270, f32[32,16,128]{2,1,0:T(8,128)} %get-tuple-element.269, f32[32,16,128]{2,1,0:T(8,128)} %get-tuple-element.268, ...), kind=kLoop, calls=%fused_computation.1099 | loop fusion | flops 4915200 | bytes 9764864 | tf_op jit(solution)/shard_map/add | solution.py:78
  184.1 3.1 %fusion.802 = f32[24,16,128]{2,1,0:T(8,128)S(1)} fusion(f32[24,16,128]{2,1,0:T(8,128)} %get-tuple-element.246, f32[32,16,128]{2,1,0:T(8,128)S(1)} %scatter-add.75, f32[24,16,128]{2,1,0:T(8,128)} %get-tuple-element.245, f32[24,16,128]{2,1,0:T(8,128)} %get-tuple-element.244, f32[24,16,128]{2,1,0:T(8,128)} %get-tuple-element.243, ...), kind=kLoop, calls=%fused_computation.1570 | loop fusion | flops 3686400 | bytes 7340032 | tf_op jit(solution)/shard_map/add | solution.py:78
  195.9 3.6 %collective-permute-start.23 = (f32[16,16,128]{2,1,0:T(8,128)S(1)}, f32[16,16,128]{2,1,0:T(8,128)S(1)}, u32[]{:S(2)}, u32[]{:S(2)}) collective-permute-start(f32[16,16,128]{2,1,0:T(8,128)S(1)} %scatter-add.79), channel_id=1, source_target_pairs={{1,0},{2,1},{3,2},{4,3},{5,4},{6,5},{7,6},{8,7},{9,8},{10,9},{11,1... | collective-permute-start | bytes 393224 | tf_op jit(solution)/shard_map/ppermute | solution.py:26
  199.6 4.2 %fusion.152 = f32[40,16,128]{2,1,0:T(8,128)S(1)} fusion(f32[40,16,128]{2,1,0:T(8,128)S(1)} %constant_dynamic-update-slice_fusion.44, f32[40,16,128]{2,1,0:T(8,128)} %get-tuple-element.296, f32[48,16,128]{2,1,0:T(8,128)S(1)} %pad_maximum_fusion, f32[40,16,128]{2,1,0:T(8,128)} %get-tuple-element.295, f32[40,16,128]{2,1,0:T(8,128)} %get-tuple-element.294, ...), kind=kLoop, calls=%fused_computation.701 | loop fusion | flops 6307840 | bytes 12189696 | tf_op jit(solution)/shard_map/add | solution.py:78
  203.9 5.3 %scatter-add.66 = f32[40,16,128]{2,1,0:T(8,128)S(1)} dynamic-update-slice(f32[40,16,128]{2,1,0:T(8,128)S(1)} %fusion.152, f32[40,16,1]{2,1,0:T(8,128)S(1)} %slice_add_fusion.1, s32[]{:T(128)} %constant.500.clone.1, s32[]{:T(128)} %constant.500.clone.1, s32[]{:T(128)} %constant.502.clone.1) | dynamic-update-slice | bytes 5124 | tf_op jit(solution)/shard_map/scatter-add | solution.py:79
  209.3 3.7 %fusion.452 = f32[32,16,128]{2,1,0:T(8,128)S(1)} fusion(f32[32,16,128]{2,1,0:T(8,128)} %get-tuple-element.271, f32[40,16,128]{2,1,0:T(8,128)S(1)} %scatter-add.66, f32[32,16,128]{2,1,0:T(8,128)} %get-tuple-element.270, f32[32,16,128]{2,1,0:T(8,128)} %get-tuple-element.269, f32[32,16,128]{2,1,0:T(8,128)} %get-tuple-element.268, ...), kind=kLoop, calls=%fused_computation.1049 | loop fusion | flops 4915200 | bytes 9764864 | tf_op jit(solution)/shard_map/add | solution.py:78
  213.9 3.3 %scatter-add.69 = f32[32,16,128]{2,1,0:T(8,128)S(1)} dynamic-update-slice(f32[32,16,128]{2,1,0:T(8,128)S(1)} %fusion.452, f32[32,16,1]{2,1,0:T(8,128)} %slice_add_fusion.13, s32[]{:T(128)} %constant.500.clone.1, s32[]{:T(128)} %constant.500.clone.1, s32[]{:T(128)} %constant.502.clone.1) | dynamic-update-slice | bytes 4100 | tf_op jit(solution)/shard_map/scatter-add | solution.py:79
  217.3 2.8 %fusion.752 = f32[24,16,128]{2,1,0:T(8,128)S(1)} fusion(f32[24,16,128]{2,1,0:T(8,128)} %get-tuple-element.246, f32[32,16,128]{2,1,0:T(8,128)S(1)} %scatter-add.69, f32[24,16,128]{2,1,0:T(8,128)} %get-tuple-element.245, f32[24,16,128]{2,1,0:T(8,128)} %get-tuple-element.244, f32[24,16,128]{2,1,0:T(8,128)} %get-tuple-element.243, ...), kind=kLoop, calls=%fused_computation.1520 | loop fusion | flops 3686400 | bytes 7340032 | tf_op jit(solution)/shard_map/add | solution.py:78
  233.1 3.9 %collective-permute-done.22 = f32[16,16,128]{2,1,0:T(8,128)S(1)} collective-permute-done((f32[16,16,128]{2,1,0:T(8,128)S(1)}, f32[16,16,128]{2,1,0:T(8,128)S(1)}, u32[]{:S(2)}, u32[]{:S(2)}) %collective-permute-start.22) | collective-permute-done | bytes 131104 | tf_op jit(solution)/shard_map/ppermute | solution.py:24
  238.0 3.1 %add_add_fusion = f32[33,16,16,128]{3,2,1,0:T(8,128)} fusion(f32[33,16,16,128]{3,2,1,0:T(8,128)S(1)} %constant_dynamic-update-slice_fusion.90, f32[33,16,16,128]{3,2,1,0:T(8,128)S(1)} %bitcast.425, f32[33,16,16,128]{3,2,1,0:T(8,128)S(1)} %constant_dynamic-update-slice_fusion.57), kind=kLoop, calls=%fused_computation.160 | loop fusion | flops 2162688 | bytes 17301504 | tf_op jit(solution)/shard_map/add | solution.py:130
  (415 shorter events, 98.9 us)
Async XLA Ops:
  0.0 57.1 %copy-start = (f32[16,16,128]{2,1,0:T(8,128)S(1)}, f32[16,16,128]{2,1,0:T(8,128)}, u32[]{:S(2)}) copy-start(f32[16,16,128]{2,1,0:T(8,128)} %param.47) | copy-start | bytes 393220
  0.0 61.9 %collective-permute-start.1 = (f32[16,16,128]{2,1,0:T(8,128)}, f32[16,16,128]{2,1,0:T(8,128)S(1)}, u32[]{:S(2)}, u32[]{:S(2)}) collective-permute-start(f32[16,16,128]{2,1,0:T(8,128)} %param.45), channel_id=1, source_target_pairs={{0,1},{1,2},{2,3},{3,4},{4,5},{5,6},{6,7},{7,8},{8,9},{9,10},{10,1... | collective-permute-start | bytes 393224 | tf_op jit(solution)/shard_map/ppermute | solution.py:24
  2.1 68.4 %collective-permute-start.3 = (f32[16,16,128]{2,1,0:T(8,128)}, f32[16,16,128]{2,1,0:T(8,128)S(1)}, u32[]{:S(2)}, u32[]{:S(2)}) collective-permute-start(f32[16,16,128]{2,1,0:T(8,128)} %param.45), channel_id=1, source_target_pairs={{1,0},{2,1},{3,2},{4,3},{5,4},{6,5},{7,6},{8,7},{9,8},{10,9},{11,1... | collective-permute-start | bytes 393224 | tf_op jit(solution)/shard_map/ppermute | solution.py:26
  5.7 59.3 %collective-permute-start.8 = (f32[16,16,128]{2,1,0:T(8,128)}, f32[16,16,128]{2,1,0:T(8,128)S(1)}, u32[]{:S(2)}, u32[]{:S(2)}) collective-permute-start(f32[16,16,128]{2,1,0:T(8,128)} %param.48), channel_id=1, source_target_pairs={{0,1},{1,2},{2,3},{3,4},{4,5},{5,6},{6,7},{7,8},{8,9},{9,10},{10,1... | collective-permute-start | bytes 393224 | tf_op jit(solution)/shard_map/ppermute | solution.py:24
  7.6 60.0 %collective-permute-start.9 = (f32[16,16,128]{2,1,0:T(8,128)}, f32[16,16,128]{2,1,0:T(8,128)S(1)}, u32[]{:S(2)}, u32[]{:S(2)}) collective-permute-start(f32[16,16,128]{2,1,0:T(8,128)} %param.48), channel_id=1, source_target_pairs={{1,0},{2,1},{3,2},{4,3},{5,4},{6,5},{7,6},{8,7},{9,8},{10,9},{11,1... | collective-permute-start | bytes 393224 | tf_op jit(solution)/shard_map/ppermute | solution.py:26
  12.3 40.5 %collective-permute-start.6 = (f32[12,16,128]{2,1,0:T(8,128)S(1)}, f32[12,16,128]{2,1,0:T(8,128)S(1)}, u32[]{:S(2)}, u32[]{:S(2)}) collective-permute-start(f32[12,16,128]{2,1,0:T(8,128)S(1)} %get-tuple-element.327), channel_id=1, source_target_pairs={{0,1},{1,2},{2,3},{3,4},{4,5},{5,6},{6,7},{7,8},{8,9},{9,10},{10,1... | collective-permute-start | bytes 294920 | tf_op jit(solution)/shard_map/ppermute | solution.py:24
  32.5 35.1 %copy-start.90 = (f32[16,16,128]{2,1,0:T(8,128)S(1)}, f32[16,16,128]{2,1,0:T(8,128)}, u32[]{:S(2)}) copy-start(f32[16,16,128]{2,1,0:T(8,128)} %param.48) | copy-start | bytes 393220
  33.3 37.1 %copy-start.91 = (f32[16,16,128]{2,1,0:T(8,128)S(1)}, f32[16,16,128]{2,1,0:T(8,128)}, u32[]{:S(2)}) copy-start(f32[16,16,128]{2,1,0:T(8,128)} %param.45) | copy-start | bytes 393220
  37.0 40.1 %copy-start.80 = (f32[16,16,128]{2,1,0:T(8,128)S(1)}, f32[16,16,128]{2,1,0:T(8,128)}, u32[]{:S(2)}) copy-start(f32[16,16,128]{2,1,0:T(8,128)} %param.46) | copy-start | bytes 393220
  52.8 6.5 %collective-permute-start.7 = (f32[12,16,128]{2,1,0:T(8,128)S(1)}, f32[12,16,128]{2,1,0:T(8,128)S(1)}, u32[]{:S(2)}, u32[]{:S(2)}) collective-permute-start(f32[12,16,128]{2,1,0:T(8,128)S(1)} %get-tuple-element.326), channel_id=1, source_target_pairs={{1,0},{2,1},{3,2},{4,3},{5,4},{6,5},{7,6},{8,7},{9,8},{10,9},{11,1... | collective-permute-start | bytes 294920 | tf_op jit(solution)/shard_map/ppermute | solution.py:26
  59.3 41.1 %collective-permute-start.2 = (f32[16,16,128]{2,1,0:T(8,128)}, f32[16,16,128]{2,1,0:T(8,128)}, u32[]{:S(2)}, u32[]{:S(2)}) collective-permute-start(f32[16,16,128]{2,1,0:T(8,128)} %param.43), channel_id=1, source_target_pairs={{0,1},{1,2},{2,3},{3,4},{4,5},{5,6},{6,7},{7,8},{8,9},{9,10},{10,1... | collective-permute-start | bytes 393224 | tf_op jit(solution)/shard_map/ppermute | solution.py:24
  61.9 43.0 %collective-permute-start = (f32[16,16,128]{2,1,0:T(8,128)}, f32[16,16,128]{2,1,0:T(8,128)}, u32[]{:S(2)}, u32[]{:S(2)}) collective-permute-start(f32[16,16,128]{2,1,0:T(8,128)} %param.43), channel_id=1, source_target_pairs={{1,0},{2,1},{3,2},{4,3},{5,4},{6,5},{7,6},{8,7},{9,8},{10,9},{11,1... | collective-permute-start | bytes 393224 | tf_op jit(solution)/shard_map/ppermute | solution.py:26
  65.0 10.1 %collective-permute-start.12 = (f32[12,16,128]{2,1,0:T(8,128)S(1)}, f32[12,16,128]{2,1,0:T(8,128)S(1)}, u32[]{:S(2)}, u32[]{:S(2)}) collective-permute-start(f32[12,16,128]{2,1,0:T(8,128)S(1)} %get-tuple-element.325), channel_id=1, source_target_pairs={{1,0},{2,1},{3,2},{4,3},{5,4},{6,5},{7,6},{8,7},{9,8},{10,9},{11,1... | collective-permute-start | bytes 294920 | tf_op jit(solution)/shard_map/ppermute | solution.py:26
  67.6 26.3 %copy-start.42 = (f32[32,16,128]{2,1,0:T(8,128)}, f32[32,16,128]{2,1,0:T(8,128)S(1)}, u32[]{:S(2)}) copy-start(f32[32,16,128]{2,1,0:T(8,128)S(1)} %get-tuple-element.317) | copy-start | bytes 786436
  67.6 9.5 %collective-permute-start.11 = (f32[12,16,128]{2,1,0:T(8,128)S(1)}, f32[12,16,128]{2,1,0:T(8,128)S(1)}, u32[]{:S(2)}, u32[]{:S(2)}) collective-permute-start(f32[12,16,128]{2,1,0:T(8,128)S(1)} %get-tuple-element.324), channel_id=1, source_target_pairs={{0,1},{1,2},{2,3},{3,4},{4,5},{5,6},{6,7},{7,8},{8,9},{9,10},{10,1... | collective-permute-start | bytes 294920 | tf_op jit(solution)/shard_map/ppermute | solution.py:24
  69.6 24.3 %copy-start.44 = (f32[32,16,128]{2,1,0:T(8,128)}, f32[32,16,128]{2,1,0:T(8,128)S(1)}, u32[]{:S(2)}) copy-start(f32[32,16,128]{2,1,0:T(8,128)S(1)} %get-tuple-element.322) | copy-start | bytes 786436
  70.4 35.4 %collective-permute-start.5 = (f32[12,16,128]{2,1,0:T(8,128)}, f32[12,16,128]{2,1,0:T(8,128)}, u32[]{:S(2)}, u32[]{:S(2)}) collective-permute-start(f32[12,16,128]{2,1,0:T(8,128)} %get-tuple-element.316), channel_id=1, source_target_pairs={{1,0},{2,1},{3,2},{4,3},{5,4},{6,5},{7,6},{8,7},{9,8},{10,9},{11,1... | collective-permute-start | bytes 294920 | tf_op jit(solution)/shard_map/ppermute | solution.py:26
  75.1 30.7 %collective-permute-start.4 = (f32[12,16,128]{2,1,0:T(8,128)}, f32[12,16,128]{2,1,0:T(8,128)}, u32[]{:S(2)}, u32[]{:S(2)}) collective-permute-start(f32[12,16,128]{2,1,0:T(8,128)} %get-tuple-element.315), channel_id=1, source_target_pairs={{0,1},{1,2},{2,3},{3,4},{4,5},{5,6},{6,7},{7,8},{8,9},{9,10},{10,1... | collective-permute-start | bytes 294920 | tf_op jit(solution)/shard_map/ppermute | solution.py:24
  81.4 24.5 %copy-start.1 = (f32[40,16,128]{2,1,0:T(8,128)}, f32[40,16,128]{2,1,0:T(8,128)S(1)}, u32[]{:S(2)}) copy-start(f32[40,16,128]{2,1,0:T(8,128)S(1)} %get-tuple-element.273) | copy-start | bytes 983044
  134.9 21.1 %copy-start.92 = (f32[16,16,128]{2,1,0:T(8,128)S(1)}, f32[16,16,128]{2,1,0:T(8,128)}, u32[]{:S(2)}) copy-start(f32[16,16,128]{2,1,0:T(8,128)} %param.45) | copy-start | bytes 393220
  136.2 59.6 %collective-permute-start.10 = (f32[16,16,128]{2,1,0:T(8,128)S(1)}, f32[16,16,128]{2,1,0:T(8,128)S(1)}, u32[]{:S(2)}, u32[]{:S(2)}) collective-permute-start(f32[16,16,128]{2,1,0:T(8,128)S(1)} %scatter-add.59), channel_id=1, source_target_pairs={{1,0},{2,1},{3,2},{4,3},{5,4},{6,5},{7,6},{8,7},{9,8},{10,9},{11,1... | collective-permute-start | bytes 393224 | tf_op jit(solution)/shard_map/ppermute | solution.py:26
  139.9 59.6 %collective-permute-start.14 = (f32[16,16,128]{2,1,0:T(8,128)S(1)}, f32[16,16,128]{2,1,0:T(8,128)S(1)}, u32[]{:S(2)}, u32[]{:S(2)}) collective-permute-start(f32[16,16,128]{2,1,0:T(8,128)S(1)} %scatter-add.59), channel_id=1, source_target_pairs={{0,1},{1,2},{2,3},{3,4},{4,5},{5,6},{6,7},{7,8},{8,9},{9,10},{10,1... | collective-permute-start | bytes 393224 | tf_op jit(solution)/shard_map/ppermute | solution.py:24
  144.6 14.4 %collective-permute-start.15 = (f32[16,16,128]{2,1,0:T(8,128)S(1)}, f32[16,16,128]{2,1,0:T(8,128)S(1)}, u32[]{:S(2)}, u32[]{:S(2)}) collective-permute-start(f32[16,16,128]{2,1,0:T(8,128)S(1)} %scatter-add.65), channel_id=1, source_target_pairs={{1,0},{2,1},{3,2},{4,3},{5,4},{6,5},{7,6},{8,7},{9,8},{10,9},{11,1... | collective-permute-start | bytes 393224 | tf_op jit(solution)/shard_map/ppermute | solution.py:26
  148.2 15.3 %collective-permute-start.13 = (f32[16,16,128]{2,1,0:T(8,128)S(1)}, f32[16,16,128]{2,1,0:T(8,128)S(1)}, u32[]{:S(2)}, u32[]{:S(2)}) collective-permute-start(f32[16,16,128]{2,1,0:T(8,128)S(1)} %scatter-add.65), channel_id=1, source_target_pairs={{0,1},{1,2},{2,3},{3,4},{4,5},{5,6},{6,7},{7,8},{8,9},{9,10},{10,1... | collective-permute-start | bytes 393224 | tf_op jit(solution)/shard_map/ppermute | solution.py:24
  150.6 48.9 %collective-permute-start.17 = (f32[12,16,128]{2,1,0:T(8,128)}, f32[12,16,128]{2,1,0:T(8,128)}, u32[]{:S(2)}, u32[]{:S(2)}) collective-permute-start(f32[12,16,128]{2,1,0:T(8,128)} %get-tuple-element.300), channel_id=1, source_target_pairs={{1,0},{2,1},{3,2},{4,3},{5,4},{6,5},{7,6},{8,7},{9,8},{10,9},{11,1... | collective-permute-start | bytes 294920 | tf_op jit(solution)/shard_map/ppermute | solution.py:26
  159.0 6.7 %collective-permute-start.20 = (f32[12,16,128]{2,1,0:T(8,128)S(1)}, f32[12,16,128]{2,1,0:T(8,128)S(1)}, u32[]{:S(2)}, u32[]{:S(2)}) collective-permute-start(f32[12,16,128]{2,1,0:T(8,128)S(1)} %get-tuple-element.298), channel_id=1, source_target_pairs={{1,0},{2,1},{3,2},{4,3},{5,4},{6,5},{7,6},{8,7},{9,8},{10,9},{11,1... | collective-permute-start | bytes 294920 | tf_op jit(solution)/shard_map/ppermute | solution.py:26
  163.6 6.8 %collective-permute-start.19 = (f32[12,16,128]{2,1,0:T(8,128)S(1)}, f32[12,16,128]{2,1,0:T(8,128)S(1)}, u32[]{:S(2)}, u32[]{:S(2)}) collective-permute-start(f32[12,16,128]{2,1,0:T(8,128)S(1)} %get-tuple-element.297), channel_id=1, source_target_pairs={{0,1},{1,2},{2,3},{3,4},{4,5},{5,6},{6,7},{7,8},{8,9},{9,10},{10,1... | collective-permute-start | bytes 294920 | tf_op jit(solution)/shard_map/ppermute | solution.py:24
  165.8 33.8 %collective-permute-start.16 = (f32[12,16,128]{2,1,0:T(8,128)}, f32[12,16,128]{2,1,0:T(8,128)}, u32[]{:S(2)}, u32[]{:S(2)}) collective-permute-start(f32[12,16,128]{2,1,0:T(8,128)} %get-tuple-element.299), channel_id=1, source_target_pairs={{0,1},{1,2},{2,3},{3,4},{4,5},{5,6},{6,7},{7,8},{8,9},{9,10},{10,1... | collective-permute-start | bytes 294920 | tf_op jit(solution)/shard_map/ppermute | solution.py:24
  193.9 38.7 %collective-permute-start.21 = (f32[16,16,128]{2,1,0:T(8,128)S(1)}, f32[16,16,128]{2,1,0:T(8,128)S(1)}, u32[]{:S(2)}, u32[]{:S(2)}) collective-permute-start(f32[16,16,128]{2,1,0:T(8,128)S(1)} %scatter-add.79), channel_id=1, source_target_pairs={{0,1},{1,2},{2,3},{3,4},{4,5},{5,6},{6,7},{7,8},{8,9},{9,10},{10,1... | collective-permute-start | bytes 393224 | tf_op jit(solution)/shard_map/ppermute | solution.py:24
  195.9 37.2 %collective-permute-start.23 = (f32[16,16,128]{2,1,0:T(8,128)S(1)}, f32[16,16,128]{2,1,0:T(8,128)S(1)}, u32[]{:S(2)}, u32[]{:S(2)}) collective-permute-start(f32[16,16,128]{2,1,0:T(8,128)S(1)} %scatter-add.79), channel_id=1, source_target_pairs={{1,0},{2,1},{3,2},{4,3},{5,4},{6,5},{7,6},{8,7},{9,8},{10,9},{11,1... | collective-permute-start | bytes 393224 | tf_op jit(solution)/shard_map/ppermute | solution.py:26
  227.0 5.6 %collective-permute-start.18 = (f32[16,16,128]{2,1,0:T(8,128)S(1)}, f32[16,16,128]{2,1,0:T(8,128)S(1)}, u32[]{:S(2)}, u32[]{:S(2)}) collective-permute-start(f32[16,16,128]{2,1,0:T(8,128)S(1)} %scatter-add.71), channel_id=1, source_target_pairs={{1,0},{2,1},{3,2},{4,3},{5,4},{6,5},{7,6},{8,7},{9,8},{10,9},{11,1... | collective-permute-start | bytes 393224 | tf_op jit(solution)/shard_map/ppermute | solution.py:26
  229.8 7.2 %collective-permute-start.22 = (f32[16,16,128]{2,1,0:T(8,128)S(1)}, f32[16,16,128]{2,1,0:T(8,128)S(1)}, u32[]{:S(2)}, u32[]{:S(2)}) collective-permute-start(f32[16,16,128]{2,1,0:T(8,128)S(1)} %scatter-add.71), channel_id=1, source_target_pairs={{0,1},{1,2},{2,3},{3,4},{4,5},{5,6},{6,7},{7,8},{8,9},{9,10},{10,1... | collective-permute-start | bytes 393224 | tf_op jit(solution)/shard_map/ppermute | solution.py:24
  (87 other events, 721.2 us)
where the time goes:
time: 245 us; the launch traced here: 241 us
  local copies, waits for them, and re-layouts  71.6 us (29%)
  other arithmetic  71.5 us (29%)
  starting transfers between devices  70.2 us (29%)
  blocking collectives  16.5 us (7%)
  waiting for transfers between devices  7.74 us (3%)
  between operations  2.78 us (1%)
    add x16, other arithmetic, advance(): 2.0 * centre_cells - prior_field + stiff_cells * laplace(current, buoyant)  52.4 us
    scatter-add x16, local copies, waits for them, and re-layouts, advance(): return updated.at[:, :, SURFACE].add(source_term)  45.7 us
    ppermute x12, starting transfers between devices, with_halo(): lax.ppermute(head, axis, [((i + 1) % count, i) for i in range(ends)])  43.8 us
    ppermute x12, starting transfers between devices, with_halo(): lax.ppermute(tail, axis, [(i, (i + 1) % count) for i in range(ends)])  26.4 us
    all_gather x1, blocking collectives, local(): all_traces = lax.all_gather(traces, 'gx', axis=1, tiled=True)  16.5 us
    another operation x24, local copies, waits for them, and re-layouts  14.6 us
    add x16, other arithmetic, advance(): return updated.at[:, :, SURFACE].add(source_term)  7.77 us
    ppermute x12, waiting for transfers between devices, with_halo(): lax.ppermute(tail, axis, [(i, (i + 1) % count) for i in range(ends)])  5.35 us
  transfers between devices with their start and end apart: 24, of which 4 were waited for; matrix products, arithmetic and copies ran while one was open for 46% of the time, Pallas kernels for 0%

commit v1 on v0

v1 whole, which is shorter than its diff:
```python
import functools

import jax
import jax.numpy as jnp
from jax import lax
from jax.experimental import pallas as pl
from jax.experimental.pallas import tpu as pltpu
from jax.sharding import PartitionSpec as P

STEPS = 8
IMG_EVERY = 4
NOFF = 33
SURFACE = 4
HALF = 16
REACH = 4
AXIS = "gx"

stencil_weights = (1.6, -0.2, 8.0 / 315.0, -1.0 / 560.0)


def split3(x):
    hi = x.astype(jnp.bfloat16)
    rest = x - hi.astype(jnp.float32)
    mid = rest.astype(jnp.bfloat16)
    low = (rest - mid.astype(jnp.float32)).astype(jnp.bfloat16)
    return hi, mid, low


def propagate(
    count,
    s_ref, sp_ref, r_ref, rp_ref, k_ref, b_ref, wave_ref, fire_ref, shot_ref, rcell_ref, trace_ref,
    out_ref,
    lev, bx, coef, plane_s, plane_r, gathered, wpad, ipad,
    send_sem, recv_sem, bsend_sem, brecv_sem, tsend_sem, trecv_sem,
):
    me = lax.axis_index(AXIS)
    rows, lateral, depth = s_ref.shape
    H, E = HALF, REACH
    has_left, has_right = me > 0, me < count - 1
    rounds = out_ref.shape[0] - 1

    def level(n):
        return out_ref.at[n // IMG_EVERY] if n % IMG_EVERY == 0 else lev.at[n]

    barrier = pltpu.get_barrier_semaphore()

    def greet(j, c):
        @pl.when(j != me)
        def _():
            pl.semaphore_signal(barrier, inc=1, device_id={AXIS: j}, device_id_type=pl.DeviceIdType.MESH)
        return c

    lax.fori_loop(0, count, greet, 0)

    first = level(0)

    def fill(i, c):
        first[H + i, 0] = s_ref[i]
        first[H + i, 1] = r_ref[i]
        bx[E + i] = b_ref[i]
        return c

    lax.fori_loop(0, rows, fill, 0)
    zero_row = jnp.zeros((2, lateral, depth), jnp.float32)

    def blank(lo_halo):
        for n in range(STEPS + 1):
            wide = H if n % IMG_EVERY == 0 else E
            at = H - wide if lo_halo else H + rows
            target = level(n)

            def one(i, c, target=target, at=at):
                target[at + i] = zero_row
                return c

            lax.fori_loop(0, wide, one, 0)
        for i in range(E):
            bx[i if lo_halo else E + rows + i] = jnp.zeros((lateral, depth), jnp.float32)

    @pl.when(jnp.logical_not(has_left))
    def _():
        blank(True)

    @pl.when(jnp.logical_not(has_right))
    def _():
        blank(False)

    gathered[me] = trace_ref[...]
    pl.semaphore_wait(barrier, count - 1)

    def halo_copy(n, side, chunk):
        if n == STEPS and chunk == 1:
            skip, size = E, H - E
        else:
            skip, size = chunk * E, E
        if side == 0:
            src, dst, to = H + rows - skip - size, H - skip - size, me + 1
        else:
            src, dst, to = H + skip, H + rows + skip, me - 1
        ref = level(n)
        return pltpu.make_async_remote_copy(
            src_ref=ref.at[pl.ds(src, size)], dst_ref=ref.at[pl.ds(dst, size)],
            send_sem=send_sem.at[n, side, chunk], recv_sem=recv_sem.at[n, side, chunk],
            device_id={AXIS: to}, device_id_type=pl.DeviceIdType.MESH)

    def b_copy(side):
        src, dst, to = (rows, 0, me + 1) if side == 0 else (E, E + rows, me - 1)
        return pltpu.make_async_remote_copy(
            src_ref=bx.at[pl.ds(src, E)], dst_ref=bx.at[pl.ds(dst, E)],
            send_sem=bsend_sem.at[side], recv_sem=brecv_sem.at[side],
            device_id={AXIS: to}, device_id_type=pl.DeviceIdType.MESH)

    def start(make):
        @pl.when(has_right)
        def _():
            make(0).start()

        @pl.when(has_left)
        def _():
            make(1).start()

    def wait_recv(make):
        @pl.when(has_left)
        def _():
            make(0).wait_recv()

        @pl.when(has_right)
        def _():
            make(1).wait_recv()

    def wait_send(make):
        @pl.when(has_right)
        def _():
            make(0).wait_send()

        @pl.when(has_left)
        def _():
            make(1).wait_send()

    def t_send(j):
        return pltpu.make_async_remote_copy(
            src_ref=trace_ref, dst_ref=gathered.at[me],
            send_sem=tsend_sem.at[j], recv_sem=trecv_sem.at[me],
            device_id={AXIS: j}, device_id_type=pl.DeviceIdType.MESH)

    def t_recv(j):
        return pltpu.make_async_remote_copy(
            src_ref=trace_ref, dst_ref=gathered.at[j],
            send_sem=tsend_sem.at[j], recv_sem=trecv_sem.at[j],
            device_id={AXIS: j}, device_id_type=pl.DeviceIdType.MESH)

    def others(act):
        def body(j, c):
            @pl.when(j != me)
            def _():
                act(j)
            return c

        lax.fori_loop(0, count, body, 0)

    others(lambda j: t_send(j).start())
    start(b_copy)
    start(lambda side: halo_copy(0, side, 0))

    lane = lax.broadcasted_iota(jnp.int32, (lateral, depth), 1)
    cross = lax.broadcasted_iota(jnp.int32, (lateral, depth), 0)

    def flat_coefs(i, c):
        b = bx[E + i]
        stiff = k_ref[i]
        total = jnp.zeros_like(b)
        for base, axis, index, length in ((8, 0, cross, lateral), (16, 1, lane, depth)):
            for k in range(1, REACH + 1):
                for s in (1, -1):
                    inside = index < length - k if s == 1 else index >= k
                    other = jnp.where(inside, pltpu.roll(b, (-s * k) % length, axis), 0.0)
                    t = (0.5 * stencil_weights[k - 1]) * (b + other)
                    total = total + t
                    coef[base + 2 * (k - 1) + (s < 0), i] = jnp.where(inside, stiff * t, 0.0)
        coef[24, i] = total
        return c

    lax.fori_loop(0, rows, flat_coefs, 0)

    def inline_coefs(i, c):
        b = bx[E + i]
        stiff = k_ref[i]
        total = coef[24, i]
        for k in range(1, REACH + 1):
            for s in (1, -1):
                t = (0.5 * stencil_weights[k - 1]) * (b + bx[E + i + s * k])
                total = total + t
                coef[2 * (k - 1) + (s < 0), i] = stiff * t
        coef[24, i] = 2.0 - stiff * total
        return c

    lax.fori_loop(E, rows - E, inline_coefs, 0)

    cells = rows * lateral
    cell_id = lax.broadcasted_iota(jnp.int32, (cells, 128), 0) + me * cells
    quiet = jnp.zeros((128 - 3 * STEPS, 128), jnp.bfloat16)

    def spread(cell_row, amounts):
        hot = jnp.where(cell_id == cell_row, 1.0, 0.0).astype(jnp.bfloat16)
        parts = jnp.concatenate(list(split3(amounts)) + [quiet], axis=0)
        return lax.dot_general(hot, parts, (((1,), (1,)), ((), ())), preferred_element_type=jnp.float32)

    def fold(p):
        return p + pltpu.roll(p, 128 - STEPS, 1) + pltpu.roll(p, 128 - 2 * STEPS, 1)

    shots, samples = wave_ref.shape
    wpad[...] = jnp.zeros_like(wpad)
    wpad[0:shots, 0:samples] = wave_ref[...]
    ipad[...] = jnp.full(ipad.shape, -1, jnp.int32)
    ipad[0:1, 0:shots] = fire_ref[...]
    ipad[1:2, 0:shots] = shot_ref[...]
    wave_t = wpad[...].T
    delay = lax.broadcasted_iota(jnp.int32, (STEPS, 128), 0) - ipad[0:1, :]
    amounts = jnp.zeros((STEPS, 128), jnp.float32)
    for d in range(samples):
        amounts = amounts + jnp.where(delay == d, wave_t[d : d + 1, :], 0.0)
    plane_s[...] = fold(spread(ipad[1:2, :], amounts))

    others(lambda j: t_recv(j).wait_recv())
    plane_r[...] = jnp.zeros_like(plane_r)

    def absorb(j, c):
        plane_r[...] += spread(rcell_ref[pl.ds(j, 1), :], gathered[j])
        return c

    lax.fori_loop(0, count, absorb, 0)
    plane_r[...] = fold(plane_r[...])

    wait_recv(b_copy)
    lax.fori_loop(0, E, inline_coefs, 0)
    lax.fori_loop(rows - E, rows, inline_coefs, 0)

    def advance(n, lo, hi):
        now, nxt = level(n), level(n + 1)

        def one(i, c):
            at = H + i
            for f in range(2):
                v = now[at, f]
                if n == 0:
                    before = (sp_ref, rp_ref)[f][i]
                else:
                    before = level(n - 1)[at, f]
                acc = [coef[24, i] * v - before]
                for base, axis, length in ((8, 0, lateral), (16, 1, depth)):
                    part = None
                    for k in range(1, REACH + 1):
                        for s in (1, -1):
                            term = coef[base + 2 * (k - 1) + (s < 0), i] * pltpu.roll(v, (-s * k) % length, axis)
                            part = term if part is None else part + term
                    acc.append(part)
                part = None
                for k in range(1, REACH + 1):
                    for s in (1, -1):
                        term = coef[2 * (k - 1) + (s < 0), i] * now[at + s * k, f]
                        part = term if part is None else part + term
                acc.append(part)
                plane, column = (plane_s, n) if f == 0 else (plane_r, STEPS - 1 - n)
                p = plane[pl.ds(pl.multiple_of(i * lateral, lateral), lateral), :]
                p = jnp.where(lane == SURFACE, pltpu.roll(p, (SURFACE - column) % 128, 1), 0.0)
                nxt[at, f] = (acc[0] + acc[1]) + (acc[2] + acc[3]) + p
            return c

        lax.fori_loop(lo, hi, one, 0)

    sent = [(0, 0)]
    for n in range(STEPS):
        wait_recv(lambda side: halo_copy(n, side, 0))
        advance(n, 0, E)
        advance(n, rows - E, rows)
        start(lambda side: halo_copy(n + 1, side, 0))
        sent.append((n + 1, 0))
        chunk = n % IMG_EVERY
        if chunk > 0:
            imaged = n - chunk
            start(lambda side: halo_copy(imaged, side, chunk))
            sent.append((imaged, chunk))
        advance(n, E, rows - E)
    start(lambda side: halo_copy(STEPS, side, 1))
    sent.append((STEPS, 1))
    for n, chunk in sent:
        if n == STEPS or chunk > 0:
            wait_recv(lambda side: halo_copy(n, side, chunk))
    wait_send(b_copy)
    for n, chunk in sent:
        wait_send(lambda side: halo_copy(n, side, chunk))
    others(lambda j: t_send(j).wait_send())


def imaging(per, rows, levels_ref, image_ref):
    block = pl.program_id(0)
    for jj in range(per):
        shift = block * per + jj - HALF

        def one(i, c, jj=jj, shift=shift):
            total = None
            for n in range(levels_ref.shape[0]):
                product = levels_ref[n, HALF + i - shift, 0] * levels_ref[n, HALF + i + shift, 1]
                total = product if total is None else total + product
            image_ref[jj, i] = total
            return c

        lax.fori_loop(0, rows, one, 0, unroll=True)


def solution(mesh):
    count = mesh.shape[AXIS]

    def local(sf, sp, rf, rp, stiff, buoy, wavelet, fire, shot, rcell, traces):
        rows, lateral, depth = sf.shape
        rounds = STEPS // IMG_EVERY
        wide = rows + 2 * HALF
        vm = pl.BlockSpec(memory_space=pltpu.VMEM)
        levels = pl.pallas_call(
            functools.partial(propagate, count),
            out_shape=jax.ShapeDtypeStruct((rounds + 1, wide, 2, lateral, depth), jnp.float32),
            in_specs=[vm] * 11,
            out_specs=vm,
            scratch_shapes=[
                pltpu.VMEM((STEPS, wide, 2, lateral, depth), jnp.float32),
                pltpu.VMEM((rows + 2 * REACH, lateral, depth), jnp.float32),
                pltpu.VMEM((25, rows, lateral, depth), jnp.float32),
                pltpu.VMEM((rows * lateral, 128), jnp.float32),
                pltpu.VMEM((rows * lateral, 128), jnp.float32),
                pltpu.VMEM((count,) + traces.shape, jnp.float32),
                pltpu.VMEM((128, 128), jnp.float32),
                pltpu.VMEM((8, 128), jnp.int32),
                pltpu.SemaphoreType.DMA((STEPS + 1, 2, 4)),
                pltpu.SemaphoreType.DMA((STEPS + 1, 2, 4)),
                pltpu.SemaphoreType.DMA((2,)),
                pltpu.SemaphoreType.DMA((2,)),
                pltpu.SemaphoreType.DMA((count,)),
                pltpu.SemaphoreType.DMA((count,)),
            ],
            compiler_params=pltpu.CompilerParams(
                collective_id=0, has_side_effects=True, vmem_limit_bytes=40 * 1024 * 1024),
        )(sf, sp, rf, rp, stiff, buoy, wavelet, fire.reshape(1, -1), shot.reshape(1, -1),
          rcell.reshape(count, traces.shape[1]), traces)
        per = 3
        return pl.pallas_call(
            functools.partial(imaging, per, rows),
            grid=(NOFF // per,),
            out_shape=jax.ShapeDtypeStruct((NOFF, rows, lateral, depth), jnp.float32),
            in_specs=[vm],
            out_specs=pl.BlockSpec((per, rows, lateral, depth), lambda j: (j, 0, 0, 0)),
            compiler_params=pltpu.CompilerParams(vmem_limit_bytes=24 * 1024 * 1024),
        )(levels)

    placed = (
        P(("shot", AXIS), None, None),
        P(("shot", AXIS), None, None),
        P(("shot", AXIS), None, None),
        P(("shot", AXIS), None, None),
        P(AXIS, None, None),
        P(AXIS, None, None),
        P("shot", None),
        P("shot"),
        P("shot"),
        P("shot"),
        P("shot", AXIS),
    )
    return jax.shard_map(
        local, mesh=mesh, in_specs=placed, out_specs=P("shot", AXIS, None, None), check_vma=False
    )
```

time: 245 us -> 65.7 us (0.27); the launches traced: 241 us -> 65.3 us
  other arithmetic: 71.5 us -> 0 us
  starting transfers between devices: 70.2 us -> 0 us
  local copies, waits for them, and re-layouts: 71.6 us -> 8.87 us
  Pallas kernels: 0 us -> 56.4 us
  blocking collectives: 16.5 us -> 0 us
  waiting for transfers between devices: 7.74 us -> 0 us
  between operations: 2.78 us -> 0.02 us
    ppermute x24 -> x0, starting transfers between devices: 70.2 us -> none  [the longest x12 43.8 us: with_halo(): lax.ppermute(head, axis, [((i + 1) % count, i) for i in range(ends)])]
    add x33 -> x0, other arithmetic: 63.3 us -> none  [the longest x16 52.4 us: advance(): 2.0 * centre_cells - prior_field + stiff_cells * laplace(current, buoyant)]
    pallas_call x0 -> x2, Pallas kernels: none -> 56.4 us  [the longest x1 51.4 us: local(): pl.pallas_call(functools.partial(propagate, count), out_shape=jax.ShapeDt...]
    scatter-add x16 -> x0, local copies, waits for them, and re-layouts: 45.7 us -> none  [advance(): return updated.at[:, :, SURFACE].add(source_term)]
    all_gather x1 -> x0, blocking collectives: 16.5 us -> none  [local(): all_traces = lax.all_gather(traces, 'gx', axis=1, tiled=True)]
    another operation x24 -> x0, local copies, waits for them, and re-layouts: 14.6 us -> none
    ppermute x24 -> x0, waiting for transfers between devices: 7.74 us -> none  [the longest x12 5.35 us: with_halo(): lax.ppermute(tail, axis, [(i, (i + 1) % count) for i in range(ends)])]
    slice x10 -> x0, local copies, waits for them, and re-layouts: 6.53 us -> none  [the longest x4 3.37 us: with_halo(): lax.slice_in_dim(cells, cells.shape[dim] - width, cells.shape[dim], axis=...]
  transfers between devices with their start and end apart: 24 -> 0, of which waited for: 4 -> 0; matrix products, arithmetic and copies ran while one was open for 46% -> 0% of each run, Pallas kernels for 0% -> 0%
where the time goes in v1:
time: 65.7 us; the launch traced here: 65.3 us
  Pallas kernels  56.4 us (86%)
  local copies, waits for them, and re-layouts  8.87 us (14%)
    pallas_call x1, Pallas kernels, local(): pl.pallas_call(functools.partial(propagate, count), out_shape=jax.ShapeDt...  51.4 us
    unnamed x21, local copies, waits for them, and re-layouts  8.87 us
    pallas_call x1, Pallas kernels, local(): pl.pallas_call(functools.partial(imaging, per, rows), grid=(NOFF // per,)...  5.05 us

profile of v1, /device:TPU:14, one launch (start us, length us, event | category | flops | bytes accessed | tf_op | source)
XLA Modules:
  0.0 65.3 jit_solution(13661599433942852288)
XLA Ops:
  0.0 0.8 %copy.12.wave_ref = f32[16,8]{1,0:T(8,128)S(1)} copy(f32[16,8]{0,1:T(8,128)} %param.17) | data formatting | bytes 1024 | tf_op args[6]
  0.8 0.0 copy-start
  0.8 0.9 %copy-done = f32[16,16,128]{2,1,0:T(8,128)S(1)} copy-done((f32[16,16,128]{2,1,0:T(8,128)S(1)}, f32[16,16,128]{2,1,0:T(8,128)}, u32[]{:S(2)}) %copy-start) | copy-done | bytes 131096
  1.7 0.0 copy-start.1
  1.7 0.9 %copy-done.1 = f32[16,16,128]{2,1,0:T(8,128)S(1)} copy-done((f32[16,16,128]{2,1,0:T(8,128)S(1)}, f32[16,16,128]{2,1,0:T(8,128)}, u32[]{:S(2)}) %copy-start.1) | copy-done | bytes 131096
  2.6 0.0 copy-start.2
  2.6 0.9 %copy-done.2 = f32[16,16,128]{2,1,0:T(8,128)S(1)} copy-done((f32[16,16,128]{2,1,0:T(8,128)S(1)}, f32[16,16,128]{2,1,0:T(8,128)}, u32[]{:S(2)}) %copy-start.2) | copy-done | bytes 131096
  3.5 0.0 copy-start.3
  3.5 0.9 %copy-done.3 = f32[16,16,128]{2,1,0:T(8,128)S(1)} copy-done((f32[16,16,128]{2,1,0:T(8,128)S(1)}, f32[16,16,128]{2,1,0:T(8,128)}, u32[]{:S(2)}) %copy-start.3) | copy-done | bytes 131096
  4.4 0.0 copy-start.4
  4.4 0.9 %copy-done.4 = f32[16,16,128]{2,1,0:T(8,128)S(1)} copy-done((f32[16,16,128]{2,1,0:T(8,128)S(1)}, f32[16,16,128]{2,1,0:T(8,128)}, u32[]{:S(2)}) %copy-start.4) | copy-done | bytes 131096
  5.3 0.0 copy-start.5
  5.3 0.9 %copy-done.5 = f32[16,16,128]{2,1,0:T(8,128)S(1)} copy-done((f32[16,16,128]{2,1,0:T(8,128)S(1)}, f32[16,16,128]{2,1,0:T(8,128)}, u32[]{:S(2)}) %copy-start.5) | copy-done | bytes 131096
  6.2 0.0 copy-start.6
  6.2 0.7 %copy-done.6 = s32[2048]{0:T(1024)S(1)} copy-done((s32[2048]{0:T(1024)S(1)}, s32[2048]{0:T(1024)}, u32[]{:S(2)}) %copy-start.6) | copy-done | bytes 8216
  6.9 0.0 copy-start.7
  6.9 0.7 %copy-done.7 = f32[8,128]{1,0:T(8,128)S(1)} copy-done((f32[8,128]{1,0:T(8,128)S(1)}, f32[8,128]{1,0:T(8,128)}, u32[]{:S(2)}) %copy-start.7) | copy-done | bytes 4120
  7.6 0.0 copy-start.8
  7.6 0.7 copy-done.8
  8.2 0.0 copy-start.9
  8.2 0.7 copy-done.9
  8.9 51.4 %shard_map.109.levels_ref = f32[3,48,2,16,128]{4,3,2,1,0:T(8,128)S(1)} custom-call(f32[16,16,128]{2,1,0:T(8,128)S(1)} %copy-done, f32[16,16,128]{2,1,0:T(8,128)S(1)} %copy-done.1, f32[16,16,128]{2,1,0:T(8,128)S(1)} %copy-done.2, f32[16,16,128]{2,1,0:T(8,128)S(1)} %copy-done.3, f32[16,16,128]{2,1,0:T(8,128)S(1)} %copy-done.4, f32[16,16,128]{2,1,0:T(8,128)S(1)} %copy-done.5, ...), custom_call_target="tpu_custom_call" | custom-call | tf_op jit(solution)/shard_map/pallas_call | solution.py:319
  60.3 5.0 %shard_map.110 = f32[33,16,16,128]{3,2,1,0:T(8,128)} custom-call(f32[3,48,2,16,128]{4,3,2,1,0:T(8,128)S(1)} %shard_map.109.levels_ref), custom_call_target="tpu_custom_call" | custom-call | tf_op jit(solution)/shard_map/pallas_call | solution.py:345
Async XLA Ops:
  0.8 0.9 %copy-start = (f32[16,16,128]{2,1,0:T(8,128)S(1)}, f32[16,16,128]{2,1,0:T(8,128)}, u32[]{:S(2)}) copy-start(f32[16,16,128]{2,1,0:T(8,128)} %s_ref.1) | copy-start | bytes 393220
  1.7 0.9 %copy-start.1 = (f32[16,16,128]{2,1,0:T(8,128)S(1)}, f32[16,16,128]{2,1,0:T(8,128)}, u32[]{:S(2)}) copy-start(f32[16,16,128]{2,1,0:T(8,128)} %sp_ref.1) | copy-start | bytes 393220
  2.6 0.9 %copy-start.2 = (f32[16,16,128]{2,1,0:T(8,128)S(1)}, f32[16,16,128]{2,1,0:T(8,128)}, u32[]{:S(2)}) copy-start(f32[16,16,128]{2,1,0:T(8,128)} %r_ref.1) | copy-start | bytes 393220
  3.5 0.9 %copy-start.3 = (f32[16,16,128]{2,1,0:T(8,128)S(1)}, f32[16,16,128]{2,1,0:T(8,128)}, u32[]{:S(2)}) copy-start(f32[16,16,128]{2,1,0:T(8,128)} %rp_ref.1) | copy-start | bytes 393220
  4.4 0.9 %copy-start.4 = (f32[16,16,128]{2,1,0:T(8,128)S(1)}, f32[16,16,128]{2,1,0:T(8,128)}, u32[]{:S(2)}) copy-start(f32[16,16,128]{2,1,0:T(8,128)} %k_ref.1) | copy-start | bytes 393220
  5.3 0.9 %copy-start.5 = (f32[16,16,128]{2,1,0:T(8,128)S(1)}, f32[16,16,128]{2,1,0:T(8,128)}, u32[]{:S(2)}) copy-start(f32[16,16,128]{2,1,0:T(8,128)} %b_ref.1) | copy-start | bytes 393220
  6.2 0.7 %copy-start.6 = (s32[2048]{0:T(1024)S(1)}, s32[2048]{0:T(1024)}, u32[]{:S(2)}) copy-start(s32[2048]{0:T(1024)} %param.20) | copy-start | bytes 24580
  6.9 0.7 %copy-start.7 = (f32[8,128]{1,0:T(8,128)S(1)}, f32[8,128]{1,0:T(8,128)}, u32[]{:S(2)}) copy-start(f32[8,128]{1,0:T(8,128)} %trace_ref.1) | copy-start | bytes 12292
  7.6 0.7 %copy-start.8 = (s32[16]{0:T(128)S(1)}, s32[16]{0:T(128)}, u32[]{:S(2)}) copy-start(s32[16]{0:T(128)} %param.18) | copy-start | bytes 196
  8.2 0.7 %copy-start.9 = (s32[16]{0:T(128)S(1)}, s32[16]{0:T(128)}, u32[]{:S(2)}) copy-start(s32[16]{0:T(128)} %param.19) | copy-start | bytes 196

commit v2 on v1

--- a/solution.py
+++ b/solution.py
@@ -14,6 +14,8 @@
 HALF = 16
 REACH = 4
 AXIS = "gx"
+UNROLL = 4
+GROUP = 3
 
 stencil_weights = (1.6, -0.2, 8.0 / 315.0, -1.0 / 560.0)
 
@@ -28,19 +30,42 @@
 
 def propagate(
     count,
-    s_ref, sp_ref, r_ref, rp_ref, k_ref, b_ref, wave_ref, fire_ref, shot_ref, rcell_ref, trace_ref,
+    s_hbm, sp_hbm, r_hbm, rp_hbm, k_hbm, b_hbm, wave_hbm, fire_hbm, shot_hbm, rcell_hbm, trace_hbm,
     out_ref,
     lev, bx, coef, plane_s, plane_r, gathered, wpad, ipad,
-    send_sem, recv_sem, bsend_sem, brecv_sem, tsend_sem, trecv_sem,
+    prior, k_ref, wave_ref, fire_ref, shot_ref, rcell_ref, trace_ref,
+    in_sem, out_sem, send_sem, recv_sem, bsend_sem, brecv_sem, tsend_sem, trecv_sem,
 ):
     me = lax.axis_index(AXIS)
-    rows, lateral, depth = s_ref.shape
+    rows, lateral, depth = s_hbm.shape
     H, E = HALF, REACH
     has_left, has_right = me > 0, me < count - 1
-    rounds = out_ref.shape[0] - 1
 
     def level(n):
-        return out_ref.at[n // IMG_EVERY] if n % IMG_EVERY == 0 else lev.at[n]
+        return lev.at[n]
+
+    def save(n):
+        return pltpu.make_async_copy(lev.at[n], out_ref.at[n // IMG_EVERY], out_sem.at[n // IMG_EVERY])
+
+    first = level(0)
+    loads = [
+        pltpu.make_async_copy(src, dst, in_sem.at[i])
+        for i, (src, dst) in enumerate((
+            (trace_hbm, trace_ref),
+            (b_hbm, bx.at[pl.ds(E, rows)]),
+            (s_hbm, first.at[pl.ds(H, rows), 0]),
+            (r_hbm, first.at[pl.ds(H, rows), 1]),
+            (k_hbm, k_ref),
+            (wave_hbm, wave_ref),
+            (fire_hbm, fire_ref),
+            (shot_hbm, shot_ref),
+            (rcell_hbm, rcell_ref),
+            (sp_hbm, prior.at[0]),
+            (rp_hbm, prior.at[1]),
+        ))
+    ]
+    for copy in loads:
+        copy.start()
 
     barrier = pltpu.get_barrier_semaphore()
 
@@ -52,15 +77,6 @@
 
     lax.fori_loop(0, count, greet, 0)
 
-    first = level(0)
-
-    def fill(i, c):
-        first[H + i, 0] = s_ref[i]
-        first[H + i, 1] = r_ref[i]
-        bx[E + i] = b_ref[i]
-        return c
-
-    lax.fori_loop(0, rows, fill, 0)
     zero_row = jnp.zeros((2, lateral, depth), jnp.float32)
 
     def blank(lo_halo):
@@ -85,8 +101,10 @@
     def _():
         blank(False)
 
+    pl.semaphore_wait(barrier, count - 1)
+    for copy in loads:
+        copy.wait()
     gathered[me] = trace_ref[...]
-    pl.semaphore_wait(barrier, count - 1)
 
     def halo_copy(n, side, chunk):
         if n == STEPS and chunk == 1:
@@ -208,17 +226,16 @@
     def fold(p):
         return p + pltpu.roll(p, 128 - STEPS, 1) + pltpu.roll(p, 128 - 2 * STEPS, 1)
 
-    shots, samples = wave_ref.shape
+    samples, shots = wave_ref.shape
     wpad[...] = jnp.zeros_like(wpad)
-    wpad[0:shots, 0:samples] = wave_ref[...]
+    wpad[0:samples, 0:shots] = wave_ref[...]
     ipad[...] = jnp.full(ipad.shape, -1, jnp.int32)
     ipad[0:1, 0:shots] = fire_ref[...]
     ipad[1:2, 0:shots] = shot_ref[...]
-    wave_t = wpad[...].T
     delay = lax.broadcasted_iota(jnp.int32, (STEPS, 128), 0) - ipad[0:1, :]
     amounts = jnp.zeros((STEPS, 128), jnp.float32)
     for d in range(samples):
-        amounts = amounts + jnp.where(delay == d, wave_t[d : d + 1, :], 0.0)
+        amounts = amounts + jnp.where(delay == d, wpad[d : d + 1, :], 0.0)
     plane_s[...] = fold(spread(ipad[1:2, :], amounts))
 
     others(lambda j: t_recv(j).wait_recv())
@@ -235,15 +252,16 @@
     lax.fori_loop(0, E, inline_coefs, 0)
     lax.fori_loop(rows - E, rows, inline_coefs, 0)
 
-    def advance(n, lo, hi):
+    def advance(n, size, row):
         now, nxt = level(n), level(n + 1)
 
-        def one(i, c):
+        def one(q, c):
+            i = row(q)
             at = H + i
             for f in range(2):
                 v = now[at, f]
                 if n == 0:
-                    before = (sp_ref, rp_ref)[f][i]
+                    before = prior[f, i]
                 else:
                     before = level(n - 1)[at, f]
                 acc = [coef[24, i] * v - before]
@@ -266,13 +284,12 @@
                 nxt[at, f] = (acc[0] + acc[1]) + (acc[2] + acc[3]) + p
             return c
 
-        lax.fori_loop(lo, hi, one, 0)
+        lax.fori_loop(0, size, one, 0, unroll=UNROLL)
 
     sent = [(0, 0)]
     for n in range(STEPS):
         wait_recv(lambda side: halo_copy(n, side, 0))
-        advance(n, 0, E)
-        advance(n, rows - E, rows)
+        advance(n, 2 * E, lambda q: jnp.where(q < E, q, rows - 2 * E + q))
         start(lambda side: halo_copy(n + 1, side, 0))
         sent.append((n + 1, 0))
         chunk = n % IMG_EVERY
@@ -280,32 +297,53 @@
             imaged = n - chunk
             start(lambda side: halo_copy(imaged, side, chunk))
             sent.append((imaged, chunk))
-        advance(n, E, rows - E)
+        advance(n, rows - 2 * E, lambda q: q + E)
+        if n >= IMG_EVERY and chunk == 0:
+            for c in range(1, HALF // E):
+                wait_recv(lambda side: halo_copy(n - IMG_EVERY, side, c))
+            save(n - IMG_EVERY).start()
     start(lambda side: halo_copy(STEPS, side, 1))
     sent.append((STEPS, 1))
-    for n, chunk in sent:
-        if n == STEPS or chunk > 0:
-            wait_recv(lambda side: halo_copy(n, side, chunk))
+    for c in range(1, HALF // E):
+        wait_recv(lambda side: halo_copy(STEPS - IMG_EVERY, side, c))
+    save(STEPS - IMG_EVERY).start()
+    for c in range(2):
+        wait_recv(lambda side: halo_copy(STEPS, side, c))
+    save(STEPS).start()
     wait_send(b_copy)
     for n, chunk in sent:
         wait_send(lambda side: halo_copy(n, side, chunk))
     others(lambda j: t_send(j).wait_send())
-
-
-def imaging(per, rows, levels_ref, image_ref):
-    block = pl.program_id(0)
-    for jj in range(per):
-        shift = block * per + jj - HALF
-
-        def one(i, c, jj=jj, shift=shift):
-            total = None
-            for n in range(levels_ref.shape[0]):
-                product = levels_ref[n, HALF + i - shift, 0] * levels_ref[n, HALF + i + shift, 1]
-                total = product if total is None else total + product
-            image_ref[jj, i] = total
-            return c
-
-        lax.fori_loop(0, rows, one, 0, unroll=True)
+    for n in range(0, STEPS + 1, IMG_EVERY):
+        save(n).wait()
+
+
+def imaging(levels_hbm, image_hbm, levels, image, in_sem, out_sem):
+    rounds, rows = levels.shape[0], image.shape[1]
+    loads = [pltpu.make_async_copy(levels_hbm.at[n], levels.at[n], in_sem.at[n]) for n in range(rounds)]
+    for copy in loads:
+        copy.start()
+    for copy in loads:
+        copy.wait()
+    stores = []
+    for start in range(0, NOFF, GROUP):
+        for j in range(start, start + GROUP):
+            shift = j - HALF
+
+            def one(i, c, j=j, shift=shift):
+                total = None
+                for n in range(rounds):
+                    product = levels[n, HALF + i - shift, 0] * levels[n, HALF + i + shift, 1]
+                    total = product if total is None else total + product
+                image[j, i] = total
+                return c
+
+            lax.fori_loop(0, rows, one, 0, unroll=True)
+        part = pl.ds(start, GROUP)
+        stores.append(pltpu.make_async_copy(image.at[part], image_hbm.at[part], out_sem.at[start // GROUP]))
+        stores[-1].start()
+    for copy in stores:
+        copy.wait()
 
 
 def solution(mesh):
@@ -315,21 +353,29 @@
         rows, lateral, depth = sf.shape
         rounds = STEPS // IMG_EVERY
         wide = rows + 2 * HALF
-        vm = pl.BlockSpec(memory_space=pltpu.VMEM)
         levels = pl.pallas_call(
             functools.partial(propagate, count),
             out_shape=jax.ShapeDtypeStruct((rounds + 1, wide, 2, lateral, depth), jnp.float32),
-            in_specs=[vm] * 11,
-            out_specs=vm,
+            in_specs=[pl.BlockSpec(memory_space=pltpu.HBM)] * 11,
+            out_specs=pl.BlockSpec(memory_space=pltpu.HBM),
             scratch_shapes=[
-                pltpu.VMEM((STEPS, wide, 2, lateral, depth), jnp.float32),
+                pltpu.VMEM((STEPS + 1, wide, 2, lateral, depth), jnp.float32),
                 pltpu.VMEM((rows + 2 * REACH, lateral, depth), jnp.float32),
                 pltpu.VMEM((25, rows, lateral, depth), jnp.float32),
                 pltpu.VMEM((rows * lateral, 128), jnp.float32),
                 pltpu.VMEM((rows * lateral, 128), jnp.float32),
                 pltpu.VMEM((count,) + traces.shape, jnp.float32),
-                pltpu.VMEM((128, 128), jnp.float32),
+                pltpu.VMEM((wavelet.shape[1], 128), jnp.float32),
                 pltpu.VMEM((8, 128), jnp.int32),
+                pltpu.VMEM((2, rows, lateral, depth), jnp.float32),
+                pltpu.VMEM((rows, lateral, depth), jnp.float32),
+                pltpu.VMEM(wavelet.shape[::-1], jnp.float32),
+                pltpu.VMEM((1,) + fire.shape, jnp.int32),
+                pltpu.VMEM((1,) + shot.shape, jnp.int32),
+                pltpu.VMEM((count, traces.shape[1]), jnp.int32),
+                pltpu.VMEM(traces.shape, jnp.float32),
+                pltpu.SemaphoreType.DMA((11,)),
+                pltpu.SemaphoreType.DMA((rounds + 1,)),
                 pltpu.SemaphoreType.DMA((STEPS + 1, 2, 4)),
                 pltpu.SemaphoreType.DMA((STEPS + 1, 2, 4)),
                 pltpu.SemaphoreType.DMA((2,)),
@@ -338,17 +384,22 @@
                 pltpu.SemaphoreType.DMA((count,)),
             ],
             compiler_params=pltpu.CompilerParams(
-                collective_id=0, has_side_effects=True, vmem_limit_bytes=40 * 1024 * 1024),
-        )(sf, sp, rf, rp, stiff, buoy, wavelet, fire.reshape(1, -1), shot.reshape(1, -1),
+                collective_id=0, has_side_effects=True, vmem_limit_bytes=62 * 1024 * 1024),
+        )(sf, sp, rf, rp, stiff, buoy, wavelet.T, fire.reshape(1, -1), shot.reshape(1, -1),
           rcell.reshape(count, traces.shape[1]), traces)
-        per = 3
+        hbm = pl.BlockSpec(memory_space=pltpu.HBM)
         return pl.pallas_call(
-            functools.partial(imaging, per, rows),
-            grid=(NOFF // per,),
+            imaging,
             out_shape=jax.ShapeDtypeStruct((NOFF, rows, lateral, depth), jnp.float32),
-            in_specs=[vm],
-            out_specs=pl.BlockSpec((per, rows, lateral, depth), lambda j: (j, 0, 0, 0)),
-            compiler_params=pltpu.CompilerParams(vmem_limit_bytes=24 * 1024 * 1024),
+            in_specs=[hbm],
+            out_specs=hbm,
+            scratch_shapes=[
+                pltpu.VMEM(levels.shape, jnp.float32),
+                pltpu.VMEM((NOFF, rows, lateral, depth), jnp.float32),
+                pltpu.SemaphoreType.DMA((rounds + 1,)),
+                pltpu.SemaphoreType.DMA((NOFF // GROUP,)),
+            ],
+            compiler_params=pltpu.CompilerParams(vmem_limit_bytes=62 * 1024 * 1024),
         )(levels)
 
     placed = (

time: 65.7 us -> 56.2 us (0.86)
  local copies, waits for them, and re-layouts: 8.87 us -> 0 us
    unnamed x21 -> x0, local copies, waits for them, and re-layouts: 8.87 us -> none
    pallas_call x1, Pallas kernels: 5.05 us -> 3.86 us  [local(): pl.pallas_call(imaging, out_shape=jax.ShapeDtypeStruct((NOFF, rows, later...]
    pallas_call x1, Pallas kernels: 51.4 us -> 52.2 us  [local(): pl.pallas_call(functools.partial(propagate, count), out_shape=jax.ShapeDt...]
where the time goes in v2:
time: 56.2 us; the launch traced here: 56.1 us
  Pallas kernels  56.1 us (100%)
    pallas_call x1, Pallas kernels, local(): pl.pallas_call(functools.partial(propagate, count), out_shape=jax.ShapeDt...  52.2 us
    pallas_call x1, Pallas kernels, local(): pl.pallas_call(imaging, out_shape=jax.ShapeDtypeStruct((NOFF, rows, later...  3.86 us

profile of v2, /device:TPU:14, one launch (start us, length us, event | category | flops | bytes accessed | tf_op | source)
XLA Modules:
  0.0 56.1 jit_solution(10075565616591907467)
XLA Ops:
  0.0 52.2 %shard_map.109.levels_hbm = f32[3,48,2,16,128]{4,3,2,1,0:T(8,128)} custom-call(f32[16,16,128]{2,1,0:T(8,128)} %s_hbm.1, f32[16,16,128]{2,1,0:T(8,128)} %sp_hbm.1, f32[16,16,128]{2,1,0:T(8,128)} %r_hbm.1, f32[16,16,128]{2,1,0:T(8,128)} %rp_hbm.1, f32[16,16,128]{2,1,0:T(8,128)} %k_hbm.1, f32[16,16,128]{2,1,0:T(8,128)} %b_hbm.1, f32[8,16]{1,0:T(8,128)} %bitcast.5, ...), custom_call_target="tpu_custom_call" | custom-call | tf_op jit(solution)/shard_map/pallas_call | solution.py:356
  52.2 3.9 %shard_map.110 = f32[33,16,16,128]{3,2,1,0:T(8,128)} custom-call(f32[3,48,2,16,128]{4,3,2,1,0:T(8,128)} %shard_map.109.levels_hbm), custom_call_target="tpu_custom_call" | custom-call | tf_op jit(solution)/shard_map/pallas_call | solution.py:391

commit v3 on v2

--- a/solution.py
+++ b/solution.py
@@ -38,7 +38,7 @@
 ):
     me = lax.axis_index(AXIS)
     rows, lateral, depth = s_hbm.shape
-    H, E = HALF, REACH
+    H, E, D = HALF, REACH, 2 * REACH
     has_left, has_right = me > 0, me < count - 1
 
     def level(n):
@@ -52,16 +52,16 @@
         pltpu.make_async_copy(src, dst, in_sem.at[i])
         for i, (src, dst) in enumerate((
             (trace_hbm, trace_ref),
-            (b_hbm, bx.at[pl.ds(E, rows)]),
+            (b_hbm, bx.at[pl.ds(D, rows)]),
             (s_hbm, first.at[pl.ds(H, rows), 0]),
             (r_hbm, first.at[pl.ds(H, rows), 1]),
-            (k_hbm, k_ref),
+            (k_hbm, k_ref.at[pl.ds(E, rows)]),
             (wave_hbm, wave_ref),
             (fire_hbm, fire_ref),
             (shot_hbm, shot_ref),
             (rcell_hbm, rcell_ref),
-            (sp_hbm, prior.at[0]),
-            (rp_hbm, prior.at[1]),
+            (sp_hbm, prior.at[pl.ds(E, rows), 0]),
+            (rp_hbm, prior.at[pl.ds(E, rows), 1]),
         ))
     ]
     for copy in loads:
@@ -80,8 +80,8 @@
     zero_row = jnp.zeros((2, lateral, depth), jnp.float32)
 
     def blank(lo_halo):
-        for n in range(STEPS + 1):
-            wide = H if n % IMG_EVERY == 0 else E
+        for n in range(0, STEPS + 1, 2):
+            wide = H if n % IMG_EVERY == 0 else D
             at = H - wide if lo_halo else H + rows
             target = level(n)
 
@@ -90,8 +90,16 @@
                 return c
 
             lax.fori_loop(0, wide, one, 0)
-        for i in range(E):
-            bx[i if lo_halo else E + rows + i] = jnp.zeros((lateral, depth), jnp.float32)
+
+        def sides(i, c):
+            at = i if lo_halo else E + rows + i
+            prior[at] = zero_row
+            k_ref[at] = zero_row[0]
+            for part in range(2):
+                bx[(part * E + i) if lo_halo else (D + rows + part * E + i)] = zero_row[0]
+            return c
+
+        lax.fori_loop(0, E, sides, 0)
 
     @pl.when(jnp.logical_not(has_left))
     def _():
@@ -106,36 +114,29 @@
         copy.wait()
     gathered[me] = trace_ref[...]
 
-    def halo_copy(n, side, chunk):
-        if n == STEPS and chunk == 1:
-            skip, size = E, H - E
+    def shifted(ref, own, skip, size, side, send, recv):
+        if side == 0:
+            src, dst, to = own + rows - skip - size, own - skip - size, me + 1
         else:
-            skip, size = chunk * E, E
-        if side == 0:
-            src, dst, to = H + rows - skip - size, H - skip - size, me + 1
-        else:
-            src, dst, to = H + skip, H + rows + skip, me - 1
-        ref = level(n)
+            src, dst, to = own + skip, own + rows + skip, me - 1
         return pltpu.make_async_remote_copy(
             src_ref=ref.at[pl.ds(src, size)], dst_ref=ref.at[pl.ds(dst, size)],
-            send_sem=send_sem.at[n, side, chunk], recv_sem=recv_sem.at[n, side, chunk],
+            send_sem=send, recv_sem=recv,
             device_id={AXIS: to}, device_id_type=pl.DeviceIdType.MESH)
 
-    def b_copy(side):
-        src, dst, to = (rows, 0, me + 1) if side == 0 else (E, E + rows, me - 1)
-        return pltpu.make_async_remote_copy(
-            src_ref=bx.at[pl.ds(src, E)], dst_ref=bx.at[pl.ds(dst, E)],
-            send_sem=bsend_sem.at[side], recv_sem=brecv_sem.at[side],
-            device_id={AXIS: to}, device_id_type=pl.DeviceIdType.MESH)
-
-    def start(make):
-        @pl.when(has_right)
-        def _():
-            make(0).start()
-
-        @pl.when(has_left)
-        def _():
-            make(1).start()
+    def halo_copy(n, side, chunk):
+        skip, size = (0, D) if chunk == 0 else (D, H - D)
+        return shifted(level(n), H, skip, size, side, send_sem.at[n, side, chunk], recv_sem.at[n, side, chunk])
+
+    def model_copy(which, side):
+        ref, own, size = ((bx, D, D), (k_ref, E, E), (prior, E, E))[which]
+        return shifted(ref, own, 0, size, side, bsend_sem.at[which, side], brecv_sem.at[which, side])
+
+    def start(make, sides=(0, 1)):
+        for side in sides:
+            @pl.when((has_right, has_left)[side])
+            def _(side=side):
+                make(side).start()
 
     def wait_recv(make):
         @pl.when(has_left)
@@ -177,8 +178,10 @@
         lax.fori_loop(0, count, body, 0)
 
     others(lambda j: t_send(j).start())
-    start(b_copy)
+    for which in range(2):
+        start(lambda side: model_copy(which, side))
     start(lambda side: halo_copy(0, side, 0))
+    start(lambda side: model_copy(2, side))
 
     lane = lax.broadcasted_iota(jnp.int32, (lateral, depth), 1)
     cross = lax.broadcasted_iota(jnp.int32, (lateral, depth), 0)
@@ -198,7 +201,7 @@
         coef[24, i] = total
         return c
 
-    lax.fori_loop(0, rows, flat_coefs, 0)
+    lax.fori_loop(E, E + rows, flat_coefs, 0, unroll=2)
 
     def inline_coefs(i, c):
         b = bx[E + i]
@@ -212,10 +215,10 @@
         coef[24, i] = 2.0 - stiff * total
         return c
 
-    lax.fori_loop(E, rows - E, inline_coefs, 0)
-
-    cells = rows * lateral
-    cell_id = lax.broadcasted_iota(jnp.int32, (cells, 128), 0) + me * cells
+    lax.fori_loop(D, rows, inline_coefs, 0, unroll=2)
+
+    cells = (rows + D) * lateral
+    cell_id = lax.broadcasted_iota(jnp.int32, (cells, 128), 0) + (me * rows - E) * lateral
     quiet = jnp.zeros((128 - 3 * STEPS, 128), jnp.bfloat16)
 
     def spread(cell_row, amounts):
@@ -248,20 +251,33 @@
     lax.fori_loop(0, count, absorb, 0)
     plane_r[...] = fold(plane_r[...])
 
-    wait_recv(b_copy)
-    lax.fori_loop(0, E, inline_coefs, 0)
-    lax.fori_loop(rows - E, rows, inline_coefs, 0)
+    wait_recv(lambda side: model_copy(0, side))
+    wait_recv(lambda side: model_copy(1, side))
+
+    def outer(q):
+        return jnp.where(q < E, q, rows + q)
+
+    def outer_coefs(q, c):
+        flat_coefs(outer(q), c)
+        inline_coefs(outer(q), c)
+        return c
+
+    def edge_coefs(q, c):
+        return inline_coefs(jnp.where(q < E, q + E, rows - E + q), c)
+
+    lax.fori_loop(0, D, outer_coefs, 0, unroll=2)
+    lax.fori_loop(0, D, edge_coefs, 0, unroll=2)
 
     def advance(n, size, row):
         now, nxt = level(n), level(n + 1)
 
         def one(q, c):
             i = row(q)
-            at = H + i
+            at = H - E + i
             for f in range(2):
                 v = now[at, f]
                 if n == 0:
-                    before = prior[f, i]
+                    before = prior[i, f]
                 else:
                     before = level(n - 1)[at, f]
                 acc = [coef[24, i] * v - before]
@@ -287,30 +303,36 @@
         lax.fori_loop(0, size, one, 0, unroll=UNROLL)
 
     sent = [(0, 0)]
-    for n in range(STEPS):
+    half = rows // 2
+    for n in range(0, STEPS, 2):
+        advance(n, rows - D, lambda q: D + q)
         wait_recv(lambda side: halo_copy(n, side, 0))
-        advance(n, 2 * E, lambda q: jnp.where(q < E, q, rows - 2 * E + q))
-        start(lambda side: halo_copy(n + 1, side, 0))
-        sent.append((n + 1, 0))
-        chunk = n % IMG_EVERY
-        if chunk > 0:
-            imaged = n - chunk
-            start(lambda side: halo_copy(imaged, side, chunk))
-            sent.append((imaged, chunk))
-        advance(n, rows - 2 * E, lambda q: q + E)
-        if n >= IMG_EVERY and chunk == 0:
-            for c in range(1, HALF // E):
-                wait_recv(lambda side: halo_copy(n - IMG_EVERY, side, c))
-            save(n - IMG_EVERY).start()
-    start(lambda side: halo_copy(STEPS, side, 1))
-    sent.append((STEPS, 1))
-    for c in range(1, HALF // E):
-        wait_recv(lambda side: halo_copy(STEPS - IMG_EVERY, side, c))
-    save(STEPS - IMG_EVERY).start()
-    for c in range(2):
-        wait_recv(lambda side: halo_copy(STEPS, side, c))
-    save(STEPS).start()
-    wait_send(b_copy)
+        if n == 0:
+            wait_recv(lambda side: model_copy(2, side))
+        advance(n, 2 * D, lambda q: jnp.where(q < D, q, rows - D + q))
+        advance(n + 1, half, lambda q: E + q)
+        start(lambda side: halo_copy(n + 2, side, 0), (1,))
+        if n + 2 == STEPS:
+            start(lambda side: halo_copy(n + 2, side, 1), (0,))
+        advance(n + 1, rows - half, lambda q: E + half + q)
+        start(lambda side: halo_copy(n + 2, side, 0), (0,))
+        sent.append((n + 2, 0))
+        if n + 2 == STEPS:
+            start(lambda side: halo_copy(n + 2, side, 1), (1,))
+            sent.append((n + 2, 1))
+        if n % IMG_EVERY == 0:
+            start(lambda side: halo_copy(n, side, 1))
+            sent.append((n, 1))
+        elif n > IMG_EVERY:
+            wait_recv(lambda side: halo_copy(0, side, 1))
+            save(0).start()
+    for n in range(IMG_EVERY, STEPS + 1, IMG_EVERY):
+        if n == STEPS:
+            wait_recv(lambda side: halo_copy(n, side, 0))
+        wait_recv(lambda side: halo_copy(n, side, 1))
+        save(n).start()
+    for which in range(3):
+        wait_send(lambda side: model_copy(which, side))
     for n, chunk in sent:
         wait_send(lambda side: halo_copy(n, side, chunk))
     others(lambda j: t_send(j).wait_send())
@@ -360,15 +382,15 @@
             out_specs=pl.BlockSpec(memory_space=pltpu.HBM),
             scratch_shapes=[
                 pltpu.VMEM((STEPS + 1, wide, 2, lateral, depth), jnp.float32),
-                pltpu.VMEM((rows + 2 * REACH, lateral, depth), jnp.float32),
-                pltpu.VMEM((25, rows, lateral, depth), jnp.float32),
-                pltpu.VMEM((rows * lateral, 128), jnp.float32),
-                pltpu.VMEM((rows * lateral, 128), jnp.float32),
+                pltpu.VMEM((rows + 4 * REACH, lateral, depth), jnp.float32),
+                pltpu.VMEM((25, rows + 2 * REACH, lateral, depth), jnp.float32),
+                pltpu.VMEM(((rows + 2 * REACH) * lateral, 128), jnp.float32),
+                pltpu.VMEM(((rows + 2 * REACH) * lateral, 128), jnp.float32),
                 pltpu.VMEM((count,) + traces.shape, jnp.float32),
                 pltpu.VMEM((wavelet.shape[1], 128), jnp.float32),
                 pltpu.VMEM((8, 128), jnp.int32),
-                pltpu.VMEM((2, rows, lateral, depth), jnp.float32),
-                pltpu.VMEM((rows, lateral, depth), jnp.float32),
+                pltpu.VMEM((rows + 2 * REACH, 2, lateral, depth), jnp.float32),
+                pltpu.VMEM((rows + 2 * REACH, lateral, depth), jnp.float32),
                 pltpu.VMEM(wavelet.shape[::-1], jnp.float32),
                 pltpu.VMEM((1,) + fire.shape, jnp.int32),
                 pltpu.VMEM((1,) + shot.shape, jnp.int32),
@@ -376,10 +398,10 @@
                 pltpu.VMEM(traces.shape, jnp.float32),
                 pltpu.SemaphoreType.DMA((11,)),
                 pltpu.SemaphoreType.DMA((rounds + 1,)),
-                pltpu.SemaphoreType.DMA((STEPS + 1, 2, 4)),
-                pltpu.SemaphoreType.DMA((STEPS + 1, 2, 4)),
-                pltpu.SemaphoreType.DMA((2,)),
-                pltpu.SemaphoreType.DMA((2,)),
+                pltpu.SemaphoreType.DMA((STEPS + 1, 2, 2)),
+                pltpu.SemaphoreType.DMA((STEPS + 1, 2, 2)),
+                pltpu.SemaphoreType.DMA((3, 2)),
+                pltpu.SemaphoreType.DMA((3, 2)),
                 pltpu.SemaphoreType.DMA((count,)),
                 pltpu.SemaphoreType.DMA((count,)),
             ],

time: 56.2 us -> 47.8 us (0.85)
  Pallas kernels: 56.1 us -> 47.3 us
    pallas_call x1, Pallas kernels: 52.2 us -> 43.4 us  [local(): pl.pallas_call(functools.partial(propagate, count), out_shape=jax.ShapeDt...]
where the time goes in v3:
time: 47.8 us; the launch traced here: 47.3 us
  Pallas kernels  47.3 us (99%)
    pallas_call x1, Pallas kernels, local(): pl.pallas_call(functools.partial(propagate, count), out_shape=jax.ShapeDt...  43.4 us
    pallas_call x1, Pallas kernels, local(): pl.pallas_call(imaging, out_shape=jax.ShapeDtypeStruct((NOFF, rows, later...  3.86 us

profile of v3, /device:TPU:14, one launch (start us, length us, event | category | flops | bytes accessed | tf_op | source)
XLA Modules:
  0.0 47.3 jit_solution(12397743846662680087)
XLA Ops:
  0.0 43.4 %shard_map.109.levels_hbm = f32[3,48,2,16,128]{4,3,2,1,0:T(8,128)} custom-call(f32[16,16,128]{2,1,0:T(8,128)} %s_hbm.1, f32[16,16,128]{2,1,0:T(8,128)} %sp_hbm.1, f32[16,16,128]{2,1,0:T(8,128)} %r_hbm.1, f32[16,16,128]{2,1,0:T(8,128)} %rp_hbm.1, f32[16,16,128]{2,1,0:T(8,128)} %k_hbm.1, f32[16,16,128]{2,1,0:T(8,128)} %b_hbm.1, f32[8,16]{1,0:T(8,128)} %bitcast.5, ...), custom_call_target="tpu_custom_call" | custom-call | tf_op jit(solution)/shard_map/pallas_call | solution.py:378
  43.4 3.9 %shard_map.110 = f32[33,16,16,128]{3,2,1,0:T(8,128)} custom-call(f32[3,48,2,16,128]{4,3,2,1,0:T(8,128)} %shard_map.109.levels_hbm), custom_call_target="tpu_custom_call" | custom-call | tf_op jit(solution)/shard_map/pallas_call | solution.py:413

commit v4 on v3

--- a/solution.py
+++ b/solution.py
@@ -1,4 +1,5 @@
 import functools
+import math
 
 import jax
 import jax.numpy as jnp
@@ -244,11 +245,18 @@
     others(lambda j: t_recv(j).wait_recv())
     plane_r[...] = jnp.zeros_like(plane_r)
 
-    def absorb(j, c):
-        plane_r[...] += spread(rcell_ref[pl.ds(j, 1), :], gathered[j])
+    batch = math.gcd(count, 4)
+
+    def absorb(q, c):
+        total = None
+        for part in range(batch):
+            j = q * batch + part
+            piece = spread(rcell_ref[pl.ds(j, 1), :], gathered[j])
+            total = piece if total is None else total + piece
+        plane_r[...] += total
         return c
 
-    lax.fori_loop(0, count, absorb, 0)
+    lax.fori_loop(0, count // batch, absorb, 0)
     plane_r[...] = fold(plane_r[...])
 
     wait_recv(lambda side: model_copy(0, side))

time: 47.8 us -> 46.5 us (0.973)
  Pallas kernels: 47.3 us -> 46.3 us
    pallas_call x1, Pallas kernels: 43.4 us -> 42.4 us  [local(): pl.pallas_call(functools.partial(propagate, count), out_shape=jax.ShapeDt...]
where the time goes in v4:
time: 46.5 us; the launch traced here: 46.3 us
  Pallas kernels  46.3 us (100%)
    pallas_call x1, Pallas kernels, local(): pl.pallas_call(functools.partial(propagate, count), out_shape=jax.ShapeDt...  42.4 us
    pallas_call x1, Pallas kernels, local(): pl.pallas_call(imaging, out_shape=jax.ShapeDtypeStruct((NOFF, rows, later...  3.86 us

profile of v4, /device:TPU:14, one launch (start us, length us, event | category | flops | bytes accessed | tf_op | source)
XLA Modules:
  0.0 46.3 jit_solution(5227168258091056206)
XLA Ops:
  0.0 42.4 %shard_map.109.levels_hbm = f32[3,48,2,16,128]{4,3,2,1,0:T(8,128)} custom-call(f32[16,16,128]{2,1,0:T(8,128)} %s_hbm.1, f32[16,16,128]{2,1,0:T(8,128)} %sp_hbm.1, f32[16,16,128]{2,1,0:T(8,128)} %r_hbm.1, f32[16,16,128]{2,1,0:T(8,128)} %rp_hbm.1, f32[16,16,128]{2,1,0:T(8,128)} %k_hbm.1, f32[16,16,128]{2,1,0:T(8,128)} %b_hbm.1, f32[8,16]{1,0:T(8,128)} %bitcast.5, ...), custom_call_target="tpu_custom_call" | custom-call | tf_op jit(solution)/shard_map/pallas_call | solution.py:386
  42.5 3.9 %shard_map.110 = f32[33,16,16,128]{3,2,1,0:T(8,128)} custom-call(f32[3,48,2,16,128]{4,3,2,1,0:T(8,128)} %shard_map.109.levels_hbm), custom_call_target="tpu_custom_call" | custom-call | tf_op jit(solution)/shard_map/pallas_call | solution.py:421
